TPU v7x, 512 devices: a whole 4x8x8 slice. The times are simulated.
512 devices in a mesh: member: 32 (over y, z_lo), patch: 16 (over z_hi, x, core).
Axes of the slice: x: 4, y: 8, z: 8 (z_hi: 2, z_lo: 4; z = z_hi * 4 + z_lo), core: 2. Of those that a mesh axis runs over, the one named last changes fastest.
Arguments:
- state_field: bfloat16 [32, 16, 256, 512], P('member', None, 'patch'), may hold values from -6 to 6
- cotangent: bfloat16 [32, 16, 256, 512], P('member', None, 'patch'), may hold values from -6 to 6
- obs_count: int32 [16, 256], P(None, 'patch'), may hold values from 0 to 4
- member_gain: float32 [512], replicated, may hold values from 0.5 to 1.5
- spatial_gain: float32 [512], replicated, may hold values from 0.5 to 1.5
- member_weights: bfloat16 [4, 512, 512], replicated, may hold values from -1 to 1
- spatial_weights: bfloat16 [4, 512, 512], replicated, may hold values from -1 to 1
Outputs:
- field_grad: bfloat16 [32, 16, 256, 512], P('member', None, 'patch')
All inputs are finite; a program needn't handle non-finite values.
Results may differ from a plain program's by a relative error of at most 0.025.
Values may be sent and summed in bfloat16 or wider, within the bound.
No kernel may reach another device: no remote copies, remote signals or barrier semaphores. Data moves between devices by JAX's collectives and lax.ppermute only.
A program may use at most 64 MiB of HBM per device.

v0:
```python
import jax
import jax.numpy as jnp
from jax import lax
from jax.sharding import PartitionSpec as P

HEADS = 8
HD = 64
WIN = 8


epsilon = 1e-06


def extended_2(array, sides, width):
    for axis, dim in sides:
        size, length = (lax.axis_size(axis), array.shape[dim])
        up = [(i, (i + 1) % size) for i in range(size)]
        down = [(j, i) for i, j in up]
        last = lax.slice_in_dim(array, length - width, length, axis=dim)
        first = lax.slice_in_dim(array, 0, width, axis=dim)
        before = lax.ppermute(last, axis, up)
        after = lax.ppermute(first, axis, down)
        array = jnp.concatenate([before, array, after], axis=dim)
    return array


def from_behind(array, axis, by):
    length = lax.axis_size(axis)
    return lax.ppermute(array, axis, [(i, (i + by) % length) for i in range(length)])


def rms_norm(activity, scaling):
    values = activity.astype(jnp.float32)
    inverse = lax.rsqrt(jnp.mean(values * values, axis=-1, keepdims=True) + epsilon)
    return (values * inverse * scaling).astype(jnp.bfloat16)


def norm_back(activity, scaling, upstream):
    values = activity.astype(jnp.float32)
    inverse = lax.rsqrt(jnp.mean(values * values, axis=-1, keepdims=True) + epsilon)
    scaled = scaling * upstream
    inner_mean = jnp.mean(scaled * values, axis=-1, keepdims=True)
    return inverse * scaled - values * inverse * inverse * inverse * inner_mean


def project(activity, matrix):
    return jnp.dot(activity, matrix, preferred_element_type=jnp.float32)


def project_back(activity, matrix):
    return lax.dot_general(
        activity,
        matrix,
        (((activity.ndim - 1,), (1,)), ((), ())),
        preferred_element_type=jnp.float32,
    )


def attention_probs(query_rows, key_rows):
    scores = jnp.einsum(
        "bqhe,bkhe->bhqk", query_rows, key_rows, preferred_element_type=jnp.float32
    ) * HD ** (-0.5)
    return jax.nn.softmax(scores, axis=-1)


def attend_forward(query_rows, key_rows, value_rows):
    rounded = attention_probs(query_rows, key_rows).astype(jnp.bfloat16)
    return jnp.einsum(
        "bhqk,bkhe->bqhe", rounded, value_rows, preferred_element_type=jnp.float32
    ).astype(jnp.bfloat16)


def attend_back(query_rows, key_rows, value_rows, output_grad):
    probs_full = attention_probs(query_rows, key_rows)
    rounded = probs_full.astype(jnp.bfloat16)
    prob_grad = jnp.einsum(
        "bqhe,bkhe->bhqk", output_grad, value_rows, preferred_element_type=jnp.float32
    )
    value_grad = jnp.einsum(
        "bhqk,bqhe->bkhe", rounded, output_grad, preferred_element_type=jnp.float32
    )
    score_grad = probs_full * (prob_grad - jnp.sum(probs_full * prob_grad, axis=-1, keepdims=True))
    score_low = (score_grad * HD ** (-0.5)).astype(jnp.bfloat16)
    query_grad = jnp.einsum(
        "bhqk,bkhe->bqhe", score_low, key_rows, preferred_element_type=jnp.float32
    )
    key_grad = jnp.einsum(
        "bhqk,bqhe->bkhe", score_low, query_rows, preferred_element_type=jnp.float32
    )
    return (query_grad, key_grad, value_grad)


def to_points(activity):
    member_count, single, point_count, feature_count = activity.shape
    shaped = activity.reshape(member_count, point_count, HEADS, feature_count // HEADS)
    return shaped.transpose(1, 0, 2, 3)


def from_points(blocks):
    point_count, member_count, head_count, head_size = blocks.shape
    return blocks.transpose(1, 0, 2, 3).reshape(
        member_count, 1, point_count, head_count * head_size
    )


def to_windows(activity):
    member_count, row_count, col_count, feature_count = activity.shape
    shaped = activity.reshape(
        member_count, row_count // WIN, WIN, col_count // WIN, WIN, HEADS, feature_count // HEADS
    )
    return shaped.transpose(0, 1, 3, 2, 4, 5, 6).reshape(
        -1, WIN * WIN, HEADS, feature_count // HEADS
    )


def from_windows(blocks, member_count, row_count, col_count):
    head_count, head_size = (blocks.shape[2], blocks.shape[3])
    shaped = blocks.reshape(
        member_count, row_count // WIN, col_count // WIN, WIN, WIN, head_count, head_size
    )
    return shaped.transpose(0, 1, 3, 2, 4, 5, 6).reshape(
        member_count, row_count, col_count, head_count * head_size
    )


def member_forward(query_pts, key_pts, value_pts):
    attended = attend_forward(to_points(query_pts), to_points(key_pts), to_points(value_pts))
    returned = lax.all_to_all(
        from_points(attended), "member", split_axis=0, concat_axis=1, tiled=True
    )
    return (returned, query_pts, key_pts, value_pts)


def split_attend(query_two, key_ext, value_ext, attn_grad_two, margin):
    mem_count, row_count, col_count, feature_count = query_two.shape
    padding = ((0, 0), (0, 0), (margin, margin), (0, 0))
    query_ext = jnp.pad(query_two, padding)
    grad_ext = jnp.pad(attn_grad_two, padding)
    query_grad, key_grad, value_grad = attend_back(
        to_windows(query_ext), to_windows(key_ext), to_windows(value_ext), to_windows(grad_ext)
    )
    wide_count = col_count + 2 * margin
    query_grad = from_windows(query_grad, mem_count, row_count, wide_count)[
        :, :, margin : margin + col_count
    ].astype(jnp.bfloat16)
    pair_grad = jnp.stack(
        [
            from_windows(key_grad, mem_count, row_count, wide_count),
            from_windows(value_grad, mem_count, row_count, wide_count),
        ]
    )
    return (query_grad, pair_grad)


def split_finish(query_grad, pair_grad, from_west, from_east, spatial_weights, margin):
    col_count = query_grad.shape[2]
    centre = pair_grad[:, :, :, margin : margin + col_count]
    centre = centre.at[:, :, :, :margin].add(from_west)
    centre = centre.at[:, :, :, col_count - margin :].add(from_east)
    key_low = centre[0].astype(jnp.bfloat16)
    value_low = centre[1].astype(jnp.bfloat16)
    return (
        project_back(query_grad, spatial_weights[0])
        + project_back(key_low, spatial_weights[1])
        + project_back(value_low, spatial_weights[2])
    )


def body(
    state_field, cotangent, obs_count, member_gain, spatial_gain, member_weights, spatial_weights
):
    mem_count, row_count, col_count, feature_count = state_field.shape
    groups = lax.axis_size("member")
    share = row_count * col_count // groups
    margin = WIN // 2
    normed_one = rms_norm(state_field, member_gain)
    grouped = normed_one.reshape(mem_count, groups, share, feature_count)
    query_loc = project(grouped, member_weights[0]).astype(jnp.bfloat16)
    key_loc = project(grouped, member_weights[1]).astype(jnp.bfloat16)
    value_loc = project(grouped, member_weights[2]).astype(jnp.bfloat16)
    returned, query_pts, key_pts, value_pts = member_forward(
        lax.all_to_all(query_loc, "member", split_axis=1, concat_axis=0, tiled=True),
        lax.all_to_all(key_loc, "member", split_axis=1, concat_axis=0, tiled=True),
        lax.all_to_all(value_loc, "member", split_axis=1, concat_axis=0, tiled=True),
    )
    attended = returned.reshape(mem_count, row_count, col_count, feature_count)
    hidden = (state_field.astype(jnp.float32) + project(attended, member_weights[3])).astype(
        jnp.bfloat16
    )
    normed_two = rms_norm(hidden, spatial_gain)
    weighting = obs_count.astype(jnp.float32)[None, :, :, None]
    out_grad = (cotangent.astype(jnp.float32) * weighting).astype(jnp.bfloat16)
    attn_grad_two = project_back(out_grad, spatial_weights[3]).astype(jnp.bfloat16)
    query_two = project(normed_two, spatial_weights[0]).astype(jnp.bfloat16)
    key_two = project(normed_two, spatial_weights[1]).astype(jnp.bfloat16)
    value_two = project(normed_two, spatial_weights[2]).astype(jnp.bfloat16)
    extended = extended_2(jnp.stack([key_two, value_two]), (("patch", 3),), margin)
    query_grad, pair_grad = split_attend(query_two, extended[0], extended[1], attn_grad_two, margin)
    from_east = from_behind(pair_grad[:, :, :, :margin].astype(jnp.bfloat16), "patch", -1).astype(
        jnp.float32
    )
    from_west = from_behind(
        pair_grad[:, :, :, margin + col_count :].astype(jnp.bfloat16), "patch", 1
    ).astype(jnp.float32)
    normed_grad_two = split_finish(
        query_grad, pair_grad, from_west, from_east, spatial_weights, margin
    )
    hidden_grad = (
        out_grad.astype(jnp.float32) + norm_back(hidden, spatial_gain, normed_grad_two)
    ).astype(jnp.bfloat16)
    attn_grad_one = project_back(hidden_grad, member_weights[3]).astype(jnp.bfloat16)
    attn_grad_one = attn_grad_one.reshape(mem_count, groups, share, feature_count)
    grad_pts = lax.all_to_all(attn_grad_one, "member", split_axis=1, concat_axis=0, tiled=True)
    grads_one = attend_back(
        to_points(query_pts), to_points(key_pts), to_points(value_pts), to_points(grad_pts)
    )
    query_pt_low, key_pts_low, value_pts_low = [
        from_points(piece.astype(jnp.bfloat16)) for piece in grads_one
    ]
    back_query, back_key, back_value = (
        lax.all_to_all(query_pt_low, "member", split_axis=0, concat_axis=1, tiled=True),
        lax.all_to_all(key_pts_low, "member", split_axis=0, concat_axis=1, tiled=True),
        lax.all_to_all(value_pts_low, "member", split_axis=0, concat_axis=1, tiled=True),
    )
    normed_grad_one = (
        project_back(back_query, member_weights[0])
        + project_back(back_key, member_weights[1])
        + project_back(back_value, member_weights[2])
    )
    normed_grad_one = normed_grad_one.reshape(mem_count, row_count, col_count, feature_count)
    return (
        hidden_grad.astype(jnp.float32) + norm_back(state_field, member_gain, normed_grad_one)
    ).astype(jnp.bfloat16)


def solution(mesh):
    placed = (
        P("member", None, "patch", None),
        P("member", None, "patch", None),
        P(None, "patch"),
        P(),
        P(),
        P(),
        P(),
    )
    return jax.shard_map(
        body,
        mesh=mesh,
        in_specs=placed,
        out_specs=P("member", None, "patch", None),
        check_vma=False,
    )
```

profile of v0, /device:TPU:8, one launch (start us, length us, event | category | flops | bytes accessed | tf_op | source)
XLA Modules:
  0.0 245.4 jit_solution(5601922900591548601)
XLA Ops:
  2.3 2.0 fusion.40
  4.4 13.1 %all-to-all-start.2 = ((bf16[1,32,8,512]{3,2,0,1:T(8,128)(2,1)}), bf16[1,32,8,512]{3,2,0,1:T(8,128)(2,1)S(1)}, u32[]{:S(2)}, u32[]{:S(2)}) async-start(bf16[1,32,8,512]{3,2,0,1:T(8,128)(2,1)} %fusion.40), calls=%async_computation.2 | async-start | bytes 524288 | tf_op jit(solution)/shard_map/all_to_all | solution.py:183
  18.5 11.7 %all-to-all-done.2 = bf16[1,32,8,512]{3,2,0,1:T(8,128)(2,1)S(1)} async-done(((bf16[1,32,8,512]{3,2,0,1:T(8,128)(2,1)}), bf16[1,32,8,512]{3,2,0,1:T(8,128)(2,1)S(1)}, u32[]{:S(2)}, u32[]{:S(2)}) %all-to-all-start.2) | async-done | bytes 262176 | tf_op jit(solution)/shard_map/all_to_all | solution.py:183
  30.2 4.4 %all-to-all-start.1 = ((bf16[1,32,8,512]{3,2,0,1:T(8,128)(2,1)}), bf16[1,32,8,512]{3,2,0,1:T(8,128)(2,1)S(1)}, u32[]{:S(2)}, u32[]{:S(2)}) async-start(bf16[1,32,8,512]{3,2,0,1:T(8,128)(2,1)} %fusion.39), calls=%async_computation.1 | async-start | bytes 524288 | tf_op jit(solution)/shard_map/all_to_all | solution.py:182
  35.6 11.1 %all-to-all-done.1 = bf16[1,32,8,512]{3,2,0,1:T(8,128)(2,1)S(1)} async-done(((bf16[1,32,8,512]{3,2,0,1:T(8,128)(2,1)}), bf16[1,32,8,512]{3,2,0,1:T(8,128)(2,1)S(1)}, u32[]{:S(2)}, u32[]{:S(2)}) %all-to-all-start.1) | async-done | bytes 262176 | tf_op jit(solution)/shard_map/all_to_all | solution.py:182
  46.7 4.7 %all-to-all-start = ((bf16[1,32,8,512]{3,2,0,1:T(8,128)(2,1)}), bf16[1,32,8,512]{3,2,0,1:T(8,128)(2,1)S(1)}, u32[]{:S(2)}, u32[]{:S(2)}) async-start(bf16[1,32,8,512]{3,2,0,1:T(8,128)(2,1)} %fusion.38), calls=%async_computation | async-start | bytes 524288 | tf_op jit(solution)/shard_map/all_to_all | solution.py:184
  52.7 3.2 %fusion.149 = (f32[8,8,32]{2,1,0:T(8,128)S(1)}, f32[8,8,32,32]{2,3,1,0:T(8,128)}) fusion(bf16[32,8,8,64]{3,2,1,0:T(8,128)(2,1)} %reshape.342, bf16[32,8,8,64]{3,2,1,0:T(8,128)(2,1)S(1)} %reshape.341), kind=kOutput, calls=%fused_computation.172 | convolution fusion | flops 8585247 | bytes 794624 | tf_op jit(solution)/shard_map/sub | solution.py:63
  55.9 7.4 %all-to-all-done = bf16[1,32,8,512]{3,2,0,1:T(8,128)(2,1)S(1)} async-done(((bf16[1,32,8,512]{3,2,0,1:T(8,128)(2,1)}), bf16[1,32,8,512]{3,2,0,1:T(8,128)(2,1)S(1)}, u32[]{:S(2)}, u32[]{:S(2)}) %all-to-all-start) | async-done | bytes 262176 | tf_op jit(solution)/shard_map/all_to_all | solution.py:184
  64.4 1.7 fusion.30
  67.4 4.9 %all-to-all-start.3 = ((bf16[32,1,8,512]{3,2,1,0:T(8,128)(2,1)}), bf16[32,1,8,512]{3,2,1,0:T(8,128)(2,1)S(1)}, u32[]{:S(2)}, u32[]{:S(2)}) async-start(bf16[32,1,8,512]{3,2,1,0:T(8,128)(2,1)} %bitcast.17), calls=%async_computation.3 | async-start | bytes 524288 | tf_op jit(solution)/shard_map/all_to_all | solution.py:128
  72.3 1.4 fusion.44
  73.8 1.3 reshape.350
  75.1 2.2 copy.94
  77.4 6.6 %all-to-all-done.3 = bf16[32,1,8,512]{3,2,1,0:T(8,128)(2,1)S(1)} async-done(((bf16[32,1,8,512]{3,2,1,0:T(8,128)(2,1)}), bf16[32,1,8,512]{3,2,1,0:T(8,128)(2,1)S(1)}, u32[]{:S(2)}, u32[]{:S(2)}) %all-to-all-start.3) | async-done | bytes 262176 | tf_op jit(solution)/shard_map/all_to_all | solution.py:128
  86.9 7.2 %collective-permute-start.1 = (bf16[2,1,16,4,512]{4,3,2,1,0:T(4,128)(2,1)}, bf16[2,1,16,4,512]{4,3,2,1,0:T(4,128)(2,1)S(1)}, u32[]{:S(2)}, u32[]{:S(2)}) collective-permute-start(bf16[2,1,16,4,512]{4,3,2,1,0:T(4,128)(2,1)} %get-tuple-element.34), channel_id=1, source_target_pairs={{1,0},{2,1},{3,2},{4,3},{5,4},{6,5},{7,6},{8,7},{9,8},{10,9},{11,1... | collective-permute-start | bytes 393224 | tf_op jit(solution)/shard_map/ppermute | solution.py:22
  94.2 2.1 collective-permute-start
  97.3 9.4 %collective-permute-done = bf16[2,1,16,4,512]{4,3,2,1,0:T(4,128)(2,1)S(1)} collective-permute-done((bf16[2,1,16,4,512]{4,3,2,1,0:T(4,128)(2,1)}, bf16[2,1,16,4,512]{4,3,2,1,0:T(4,128)(2,1)S(1)}, u32[]{:S(2)}, u32[]{:S(2)}) %collective-permute-start) | collective-permute-done | bytes 131104 | tf_op jit(solution)/shard_map/ppermute | solution.py:21
  109.8 1.7 fusion.155
  111.5 1.8 fusion.154
  113.3 4.5 %fusion.26 = bf16[6,64,8,64]{1,3,2,0:T(8,128)(2,1)} fusion(bf16[6,64,8,64]{3,1,2,0:T(8,128)(2,1)S(1)} %bitcast.262, f32[6,8,64,64]{2,3,1,0:T(8,128)} %fusion.155, f32[6,8,64,64]{2,3,1,0:T(8,128)} %get-tuple-element.40, f32[6,8,64]{2,1,0:T(8,128)S(1)} %get-tuple-element.39), kind=kOutput, calls=%fused_computation.25 | convolution fusion | flops 26741824 | bytes 2371584 | tf_op jit(solution)/shard_map/bhqk,bkhe->bqhe/dot_general | solution.py:84
  117.8 4.7 %fusion.14 = f32[6,64,8,64]{1,3,2,0:T(8,128)} fusion(bf16[6,64,8,64]{3,1,2,0:T(8,128)(2,1)S(1)} %bitcast.260, f32[6,8,64,64]{2,3,1,0:T(8,128)} %fusion.155, f32[6,8,64,64]{2,3,1,0:T(8,128)} %get-tuple-element.40, f32[6,8,64]{2,1,0:T(8,128)S(1)} %get-tuple-element.39), kind=kOutput, calls=%fused_computation.11 | convolution fusion | flops 26545216 | bytes 2764800 | tf_op jit(solution)/shard_map/bhqk,bqhe->bkhe/dot_general | solution.py:87
  122.5 3.1 %convolution_bitcast_fusion = f32[6,64,8,64]{1,3,2,0:T(8,128)} fusion(bf16[6,64,8,64]{3,1,2,0:T(8,128)(2,1)S(1)} %bitcast.254, f32[6,8,64,64]{2,3,1,0:T(8,128)} %get-tuple-element.40, f32[6,8,64]{2,1,0:T(8,128)S(1)} %get-tuple-element.39), kind=kOutput, calls=%fused_computation.14 | convolution fusion | flops 25559040 | bytes 1978368 | tf_op jit(solution)/shard_map/bhqk,bqhe->bkhe/dot_general | solution.py:79
  125.7 1.9 copy.102
  128.9 1.8 stack_reshape.6
  130.8 3.0 %copy.106 = f32[6,64,8,64]{3,2,1,0:T(8,128)} copy(f32[6,64,8,64]{1,3,2,0:T(8,128)} %convolution_bitcast_fusion) | data formatting | bytes 1572864 | tf_op jit(solution)/shard_map/bhqk,bqhe->bkhe/transpose | solution.py:79
  133.8 2.7 %copy.107 = f32[1,2,8,3,8,8,64]{6,5,4,3,2,1,0:T(8,128)} copy(f32[1,2,8,3,8,8,64]{6,5,4,2,3,1,0:T(8,128)} %bitcast.242) | data formatting | bytes 1572864 | tf_op jit(solution)/shard_map/transpose | solution.py:121
  136.5 1.8 stack_reshape.7
  139.6 2.4 copy.98
  142.1 2.1 copy.99
  144.1 2.4 reshape.354
  147.6 1.9 collective-permute-start.2
  149.5 9.7 %collective-permute-start.3 = (bf16[2,1,16,4,512]{4,3,2,1,0:T(4,128)(2,1)S(1)}, bf16[2,1,16,4,512]{4,3,2,1,0:T(4,128)(2,1)S(1)}, u32[]{:S(2)}, u32[]{:S(2)}) collective-permute-start(bf16[2,1,16,4,512]{4,3,2,1,0:T(4,128)(2,1)S(1)} %get-tuple-element.29), channel_id=1, source_target_pairs={{0,15},{1,0},{2,1},{3,2},{4,3},{5,4},{6,5},{7,6},{8,7},{9,8},{10,9... | collective-permute-start | bytes 393224 | tf_op jit(solution)/shard_map/ppermute | solution.py:29
  159.2 1.5 fusion.70
  165.1 18.1 %all_to_all.32 = bf16[1,32,8,512]{3,2,0,1:T(8,128)(2,1)} all-to-all(bf16[1,32,8,512]{3,2,0,1:T(8,128)(2,1)S(1)} %bitcast.263), channel_id=1, replica_groups=mesh['member'=32,'patch'=16] {'member'}, dimensions={1} | all-to-all | bytes 524288 | tf_op jit(solution)/shard_map/all_to_all | solution.py:213
  183.1 1.3 reshape.360
  184.4 1.7 fusion.64
  186.1 3.9 %fusion.31 = bf16[32,8,8,64]{3,0,2,1:T(8,128)(2,1)} fusion(f32[8,8,32,32]{2,3,1,0:T(8,128)} %fusion.64, bf16[32,8,8,64]{3,2,1,0:T(8,128)(2,1)} %reshape.342, f32[8,8,32,32]{2,3,1,0:T(8,128)} %get-tuple-element.36, f32[8,8,32]{2,1,0:T(8,128)S(1)} %copy-done.21), kind=kOutput, calls=%fused_computation.29 | convolution fusion | flops 8980511 | bytes 1056768 | tf_op jit(solution)/shard_map/bhqk,bkhe->bqhe/dot_general | solution.py:84
  192.3 5.3 %all-to-all-start.5 = ((bf16[32,1,8,512]{3,2,1,0:T(8,128)(2,1)}), bf16[32,1,8,512]{3,2,1,0:T(8,128)(2,1)}, u32[]{:S(2)}, u32[]{:S(2)}) async-start(bf16[32,1,8,512]{3,2,1,0:T(8,128)(2,1)} %bitcast.257), calls=%async_computation.5 | async-start | bytes 524288 | tf_op jit(solution)/shard_map/all_to_all | solution.py:221
  197.7 4.0 %fusion.32 = bf16[32,8,8,64]{3,0,2,1:T(8,128)(2,1)} fusion(f32[8,8,32,32]{2,3,1,0:T(8,128)} %fusion.64, bf16[32,8,8,64]{3,2,1,0:T(8,128)(2,1)} %copy-done.9, f32[8,8,32,32]{2,3,1,0:T(8,128)} %get-tuple-element.36, f32[8,8,32]{2,1,0:T(8,128)S(1)} %copy-done.21), kind=kOutput, calls=%fused_computation.30 | convolution fusion | flops 8980511 | bytes 1056768 | tf_op jit(solution)/shard_map/bhqk,bqhe->bkhe/dot_general | solution.py:87
  203.9 5.3 %all-to-all-done.5 = bf16[32,1,8,512]{3,2,1,0:T(8,128)(2,1)} async-done(((bf16[32,1,8,512]{3,2,1,0:T(8,128)(2,1)}), bf16[32,1,8,512]{3,2,1,0:T(8,128)(2,1)}, u32[]{:S(2)}, u32[]{:S(2)}) %all-to-all-start.5) | async-done | bytes 262176 | tf_op jit(solution)/shard_map/all_to_all | solution.py:221
  209.2 5.4 %all-to-all-start.6 = ((bf16[32,1,8,512]{3,2,1,0:T(8,128)(2,1)}), bf16[32,1,8,512]{3,2,1,0:T(8,128)(2,1)}, u32[]{:S(2)}, u32[]{:S(2)}) async-start(bf16[32,1,8,512]{3,2,1,0:T(8,128)(2,1)} %bitcast.256), calls=%async_computation.6 | async-start | bytes 524288 | tf_op jit(solution)/shard_map/all_to_all | solution.py:222
  214.6 1.7 fusion.33
  217.5 8.5 %all-to-all-done.6 = bf16[32,1,8,512]{3,2,1,0:T(8,128)(2,1)} async-done(((bf16[32,1,8,512]{3,2,1,0:T(8,128)(2,1)}), bf16[32,1,8,512]{3,2,1,0:T(8,128)(2,1)}, u32[]{:S(2)}, u32[]{:S(2)}) %all-to-all-start.6) | async-done | bytes 262176 | tf_op jit(solution)/shard_map/all_to_all | solution.py:222
  226.1 5.5 %all-to-all-start.7 = ((bf16[32,1,8,512]{3,2,1,0:T(8,128)(2,1)}), bf16[32,1,8,512]{3,2,1,0:T(8,128)(2,1)}, u32[]{:S(2)}, u32[]{:S(2)}) async-start(bf16[32,1,8,512]{3,2,1,0:T(8,128)(2,1)} %bitcast.69), calls=%async_computation.7 | async-start | bytes 524288 | tf_op jit(solution)/shard_map/all_to_all | solution.py:223
  231.6 1.3 fusion.85
  232.9 1.3 convolution_add_fusion.1
  234.2 8.7 %all-to-all-done.7 = bf16[32,1,8,512]{3,2,1,0:T(8,128)(2,1)} async-done(((bf16[32,1,8,512]{3,2,1,0:T(8,128)(2,1)}), bf16[32,1,8,512]{3,2,1,0:T(8,128)(2,1)}, u32[]{:S(2)}, u32[]{:S(2)}) %all-to-all-start.7) | async-done | bytes 262176 | tf_op jit(solution)/shard_map/all_to_all | solution.py:223
  242.9 1.3 convolution_add_fusion
  (98 shorter events, 29.9 us)
Async XLA Ops:
  0.0 17.5 %copy-start.1 = (bf16[4,512,512]{2,1,0:T(8,128)(2,1)S(1)}, bf16[4,512,512]{2,1,0:T(8,128)(2,1)}, u32[]{:S(2)}) copy-start(bf16[4,512,512]{2,1,0:T(8,128)(2,1)} %param.16) | copy-start | bytes 6291460
  4.4 25.8 %all-to-all-start.2 = ((bf16[1,32,8,512]{3,2,0,1:T(8,128)(2,1)}), bf16[1,32,8,512]{3,2,0,1:T(8,128)(2,1)S(1)}, u32[]{:S(2)}, u32[]{:S(2)}) async-start(bf16[1,32,8,512]{3,2,0,1:T(8,128)(2,1)} %fusion.40), calls=%async_computation.2 | async-start | bytes 524288 | tf_op jit(solution)/shard_map/all_to_all | solution.py:183
  30.2 16.5 %all-to-all-start.1 = ((bf16[1,32,8,512]{3,2,0,1:T(8,128)(2,1)}), bf16[1,32,8,512]{3,2,0,1:T(8,128)(2,1)S(1)}, u32[]{:S(2)}, u32[]{:S(2)}) async-start(bf16[1,32,8,512]{3,2,0,1:T(8,128)(2,1)} %fusion.39), calls=%async_computation.1 | async-start | bytes 524288 | tf_op jit(solution)/shard_map/all_to_all | solution.py:182
  46.7 16.6 %all-to-all-start = ((bf16[1,32,8,512]{3,2,0,1:T(8,128)(2,1)}), bf16[1,32,8,512]{3,2,0,1:T(8,128)(2,1)S(1)}, u32[]{:S(2)}, u32[]{:S(2)}) async-start(bf16[1,32,8,512]{3,2,0,1:T(8,128)(2,1)} %fusion.38), calls=%async_computation | async-start | bytes 524288 | tf_op jit(solution)/shard_map/all_to_all | solution.py:184
  52.7 3.2 %copy-start.9 = (bf16[32,8,8,64]{3,2,1,0:T(8,128)(2,1)}, bf16[32,8,8,64]{3,2,1,0:T(8,128)(2,1)S(1)}, u32[]{:S(2)}) copy-start(bf16[32,8,8,64]{3,2,1,0:T(8,128)(2,1)S(1)} %reshape.341) | copy-start | bytes 786436
  55.9 7.7 %copy-start.20 = (f32[8,8,32]{2,1,0:T(8,128)}, f32[8,8,32]{2,1,0:T(8,128)S(1)}, u32[]{:S(2)}) copy-start(f32[8,8,32]{2,1,0:T(8,128)S(1)} %get-tuple-element.35) | copy-start | bytes 24580
  63.6 0.8 copy-start.4
  66.1 6.2 %copy-start.17 = (s32[16,16]{1,0:T(8,128)S(1)}, s32[16,16]{1,0:T(8,128)}, u32[]{:S(2)}) copy-start(s32[16,16]{1,0:T(8,128)} %param.13) | copy-start | bytes 3076
  66.1 6.2 %copy-start.12 = (bf16[1,16,16,512]{3,2,1,0:T(8,128)(2,1)S(1)}, bf16[1,16,16,512]{3,2,1,0:T(8,128)(2,1)}, u32[]{:S(2)}) copy-start(bf16[1,16,16,512]{3,2,1,0:T(8,128)(2,1)} %param.12) | copy-start | bytes 786436
  67.4 16.6 %all-to-all-start.3 = ((bf16[32,1,8,512]{3,2,1,0:T(8,128)(2,1)}), bf16[32,1,8,512]{3,2,1,0:T(8,128)(2,1)S(1)}, u32[]{:S(2)}, u32[]{:S(2)}) async-start(bf16[32,1,8,512]{3,2,1,0:T(8,128)(2,1)} %bitcast.17), calls=%async_computation.3 | async-start | bytes 524288 | tf_op jit(solution)/shard_map/all_to_all | solution.py:128
  72.3 5.1 %copy-start.14 = (f32[16,16]{1,0:T(8,128)}, f32[16,16]{1,0:T(8,128)S(1)}, u32[]{:S(2)}) copy-start(f32[16,16]{1,0:T(8,128)S(1)} %convert_element_type.149) | copy-start | bytes 3076
  73.7 10.2 %copy-start = (bf16[1,16,16,512]{3,2,1,0:T(8,128)(2,1)S(1)}, bf16[1,16,16,512]{3,2,1,0:T(8,128)(2,1)}, u32[]{:S(2)}) copy-start(bf16[1,16,16,512]{3,2,1,0:T(8,128)(2,1)} %param.11) | copy-start | bytes 786436
  75.1 9.2 %copy-start.18 = (f32[512]{0:T(512)S(1)}, f32[512]{0:T(512)}, u32[]{:S(2)}) copy-start(f32[512]{0:T(512)} %param.15) | copy-start | bytes 6148
  83.9 1.6 copy-start.10
  86.9 10.3 %collective-permute-start.1 = (bf16[2,1,16,4,512]{4,3,2,1,0:T(4,128)(2,1)}, bf16[2,1,16,4,512]{4,3,2,1,0:T(4,128)(2,1)S(1)}, u32[]{:S(2)}, u32[]{:S(2)}) collective-permute-start(bf16[2,1,16,4,512]{4,3,2,1,0:T(4,128)(2,1)} %get-tuple-element.34), channel_id=1, source_target_pairs={{1,0},{2,1},{3,2},{4,3},{5,4},{6,5},{7,6},{8,7},{9,8},{10,9},{11,1... | collective-permute-start | bytes 393224 | tf_op jit(solution)/shard_map/ppermute | solution.py:22
  94.2 12.5 %collective-permute-start = (bf16[2,1,16,4,512]{4,3,2,1,0:T(4,128)(2,1)}, bf16[2,1,16,4,512]{4,3,2,1,0:T(4,128)(2,1)S(1)}, u32[]{:S(2)}, u32[]{:S(2)}) collective-permute-start(bf16[2,1,16,4,512]{4,3,2,1,0:T(4,128)(2,1)} %get-tuple-element.33), channel_id=1, source_target_pairs={{0,1},{1,2},{2,3},{3,4},{4,5},{5,6},{6,7},{7,8},{8,9},{9,10},{10,1... | collective-permute-start | bytes 393224 | tf_op jit(solution)/shard_map/ppermute | solution.py:21
  108.7 1.1 copy-start.3
  109.8 1.7 copy-start.8
  147.6 13.1 %collective-permute-start.2 = (bf16[2,1,16,4,512]{4,3,2,1,0:T(4,128)(2,1)S(1)}, bf16[2,1,16,4,512]{4,3,2,1,0:T(4,128)(2,1)S(1)}, u32[]{:S(2)}, u32[]{:S(2)}) collective-permute-start(bf16[2,1,16,4,512]{4,3,2,1,0:T(4,128)(2,1)S(1)} %get-tuple-element.30), channel_id=1, source_target_pairs={{0,1},{1,2},{2,3},{3,4},{4,5},{5,6},{6,7},{7,8},{8,9},{9,10},{10,1... | collective-permute-start | bytes 393224 | tf_op jit(solution)/shard_map/ppermute | solution.py:29
  149.5 12.2 %collective-permute-start.3 = (bf16[2,1,16,4,512]{4,3,2,1,0:T(4,128)(2,1)S(1)}, bf16[2,1,16,4,512]{4,3,2,1,0:T(4,128)(2,1)S(1)}, u32[]{:S(2)}, u32[]{:S(2)}) collective-permute-start(bf16[2,1,16,4,512]{4,3,2,1,0:T(4,128)(2,1)S(1)} %get-tuple-element.29), channel_id=1, source_target_pairs={{0,15},{1,0},{2,1},{3,2},{4,3},{5,4},{6,5},{7,6},{8,7},{9,8},{10,9... | collective-permute-start | bytes 393224 | tf_op jit(solution)/shard_map/ppermute | solution.py:29
  160.7 1.6 copy-start.11
  161.9 0.8 copy-start.19
  162.7 0.9 copy-start.13
  162.7 1.0 copy-start.15
  162.7 1.7 copy-start.2
  164.4 0.7 copy-start.6
  164.4 20.0 %copy-start.5 = (bf16[32,8,8,64]{3,2,1,0:T(8,128)(2,1)S(1)}, bf16[32,8,8,64]{3,2,1,0:T(8,128)(2,1)}, u32[]{:S(2)}) copy-start(bf16[32,8,8,64]{3,2,1,0:T(8,128)(2,1)} %copy-done.4) | copy-start | bytes 786436
  165.1 21.1 %copy-start.21 = (f32[8,8,32]{2,1,0:T(8,128)S(1)}, f32[8,8,32]{2,1,0:T(8,128)}, u32[]{:S(2)}) copy-start(f32[8,8,32]{2,1,0:T(8,128)} %copy-done.20) | copy-start | bytes 24580
  192.3 16.9 %all-to-all-start.5 = ((bf16[32,1,8,512]{3,2,1,0:T(8,128)(2,1)}), bf16[32,1,8,512]{3,2,1,0:T(8,128)(2,1)}, u32[]{:S(2)}, u32[]{:S(2)}) async-start(bf16[32,1,8,512]{3,2,1,0:T(8,128)(2,1)} %bitcast.257), calls=%async_computation.5 | async-start | bytes 524288 | tf_op jit(solution)/shard_map/all_to_all | solution.py:221
  209.2 16.9 %all-to-all-start.6 = ((bf16[32,1,8,512]{3,2,1,0:T(8,128)(2,1)}), bf16[32,1,8,512]{3,2,1,0:T(8,128)(2,1)}, u32[]{:S(2)}, u32[]{:S(2)}) async-start(bf16[32,1,8,512]{3,2,1,0:T(8,128)(2,1)} %bitcast.256), calls=%async_computation.6 | async-start | bytes 524288 | tf_op jit(solution)/shard_map/all_to_all | solution.py:222
  226.1 16.9 %all-to-all-start.7 = ((bf16[32,1,8,512]{3,2,1,0:T(8,128)(2,1)}), bf16[32,1,8,512]{3,2,1,0:T(8,128)(2,1)}, u32[]{:S(2)}, u32[]{:S(2)}) async-start(bf16[32,1,8,512]{3,2,1,0:T(8,128)(2,1)} %bitcast.69), calls=%async_computation.7 | async-start | bytes 524288 | tf_op jit(solution)/shard_map/all_to_all | solution.py:223
  232.9 11.4 %copy-start.16 = (f32[512]{0:T(512)S(1)}, f32[512]{0:T(512)}, u32[]{:S(2)}) copy-start(f32[512]{0:T(512)} %param.14) | copy-start | bytes 6148
  242.9 1.5 copy-start.7
where the time goes:
time: 247 us; the launch traced here: 245 us
  waiting for transfers between devices  69.5 us (28%)
  starting transfers between devices  64.2 us (26%)
  matrix products  45.2 us (18%)
  local copies, waits for them, and re-layouts  41.3 us (17%)
  blocking collectives  18.1 us (7%)
  other arithmetic  6.4 us (3%)
    all_to_all x1, blocking collectives, body(): lax.all_to_all(attn_grad_one, 'member', split_axis=1, concat_axis=0, tile...  18.1 us
    all_to_all x1, starting transfers between devices, body(): lax.all_to_all(key_loc, 'member', split_axis=1, concat_axis=0, tiled=True)  13.1 us
    all_to_all x1, waiting for transfers between devices, body(): lax.all_to_all(key_loc, 'member', split_axis=1, concat_axis=0, tiled=True)  11.7 us
    ppermute x2, starting transfers between devices, from_behind(): lax.ppermute(array, axis, [(i, (i + by) % length) for i in range(length)])  11.6 us
    all_to_all x1, waiting for transfers between devices, body(): lax.all_to_all(query_loc, 'member', split_axis=1, concat_axis=0, tiled=True)  11.1 us
    ppermute x1, waiting for transfers between devices, extended_2(): before = lax.ppermute(last, axis, up)  9.4 us
    all_to_all x1, waiting for transfers between devices, body(): lax.all_to_all(value_pts_low, 'member', split_axis=0, concat_axis=1, tile...  8.74 us
    dot_general x2, matrix products, attend_back(): jnp.einsum('bhqk,bqhe->bkhe', score_low, query_rows, preferred_element_ty...  8.71 us
  transfers between devices with their start and end apart: 11, of which 9 were waited for; matrix products, arithmetic and copies ran while one was open for 11% of the time, Pallas kernels for 0%

commit v1 on v0

v1 whole, which is shorter than its diff:
```python
import jax
import jax.numpy as jnp
from jax import lax
from jax.experimental import pallas as pl
from jax.experimental.pallas import tpu as pltpu
from jax.sharding import PartitionSpec as P

F32 = jnp.float32
BF16 = jnp.bfloat16
D = 512
PAIRS = 4
SCALE = 64 ** (-0.5)
EPS = 1e-6
ROWS = 256
BLOCK = 128

NN = (((1,), (0,)), ((), ()))
NT = (((1,), (1,)), ((), ()))
TN = (((0,), (0,)), ((), ()))


def dot(a, b, dims=NN):
    return lax.dot_general(a, b, dims, preferred_element_type=F32)


def inverse_rms(values):
    return lax.rsqrt(jnp.mean(values * values, axis=-1, keepdims=True) + EPS)


def norm_back(values, inverse, gain, upstream):
    scaled = gain * upstream
    inner = jnp.mean(scaled * values, axis=-1, keepdims=True)
    return inverse * scaled - values * (inverse * inverse * inverse * inner)


def cell_major():
    to = lax.broadcasted_iota(jnp.int32, (ROWS, ROWS), 0)
    at = lax.broadcasted_iota(jnp.int32, (ROWS, ROWS), 1)
    return (at == (to % 32) * 8 + to // 32).astype(F32).astype(BF16)


def member_major():
    to = lax.broadcasted_iota(jnp.int32, (ROWS, ROWS), 0)
    at = lax.broadcasted_iota(jnp.int32, (ROWS, ROWS), 1)
    return (at == (to % 8) * 32 + to // 8).astype(F32).astype(BF16)


def head_split(rows):
    first = lax.broadcasted_iota(jnp.int32, rows.shape, 1) < 64
    zero = jnp.zeros_like(rows)
    return jnp.concatenate([jnp.where(first, rows, zero), jnp.where(first, zero, rows)], axis=0)


def head_join(stacked):
    first = lax.broadcasted_iota(jnp.int32, (BLOCK, 128), 1) < 64
    return jnp.where(first, stacked[:BLOCK], stacked[BLOCK:])


def own_group(width, size):
    return (lax.broadcasted_iota(jnp.int32, (size, width), 1) % BLOCK) // size


def compact(full, size):
    group = own_group(full.shape[1], size)
    kept = full[:size]
    for g in range(1, BLOCK // size):
        kept = jnp.where(group == g, full[g * size : (g + 1) * size], kept)
    return kept


def expand(kept, size):
    group = own_group(kept.shape[1], size)
    zero = jnp.zeros_like(kept)
    return jnp.concatenate(
        [jnp.where(group == g, kept, zero) for g in range(BLOCK // size)], axis=0
    ).astype(BF16)


def softmax_keys(scores):
    raised = jnp.exp(scores - jnp.max(scores, axis=0, keepdims=True))
    return raised * (1.0 / jnp.sum(raised, axis=0, keepdims=True))


def block_backward(probs, q_two, k, v, do_two, size):
    grad = compact(dot(v, do_two, NT), size)
    inner = jnp.sum(probs * grad, axis=0, keepdims=True)
    ds = expand(probs * (grad - inner) * SCALE, size)
    dv = dot(expand(probs, size), do_two)
    dk = dot(ds, q_two)
    dq = head_join(dot(ds, k, TN))
    return dq, dk, dv


def spread_kernel(state_ref, cot_ref, obs_ref, out_ref):
    obs = obs_ref[...].astype(F32)
    eye = lax.broadcasted_iota(jnp.int32, (16, 16, 16), 1) == lax.broadcasted_iota(
        jnp.int32, (16, 16, 16), 2
    )
    weight = jnp.sum(jnp.where(eye, obs[:, None, :], 0.0), axis=-1, keepdims=True)
    dy = cot_ref[...].astype(F32) * weight
    parts = []
    for values in (state_ref[...].astype(F32), dy):
        inner = values[:, 4:12]
        west = values[:, 0:4].reshape(8, 2, 4, D)
        east = values[:, 12:16].reshape(8, 2, 4, D)
        parts.append(
            [
                jnp.concatenate([west[:, 0], west[:, 1]], axis=1),
                inner,
                jnp.concatenate([east[:, 0], east[:, 1]], axis=1),
            ]
        )
    for at, size, a, b in zip((0, 8, 24), (8, 16, 8), parts[0], parts[1]):
        out_ref[at : at + size] = jnp.concatenate([a, b], axis=1).astype(BF16)


def gather_kernel(in_ref, out_ref):
    values = in_ref[...].astype(F32)
    west, east = values[0:8], values[24:32]
    inner = values[8:24].reshape(8, 2, 8, D)
    rows = [
        jnp.concatenate([west[:, 4 * i : 4 * i + 4], inner[:, i], east[:, 4 * i : 4 * i + 4]], axis=1)
        for i in range(2)
    ]
    out_ref[...] = jnp.stack(rows, axis=1).reshape(16, 16, D).astype(BF16)


def member_forward_kernel(
    in_ref, gain_ref, w_ref, out_ref, state_ref, q_ref, k_ref, v_ref, probs_ref, attended_ref
):
    values = in_ref[...].astype(F32)
    state = dot(cell_major(), values[:, :8].reshape(ROWS, D).astype(BF16))
    state_ref[...] = state.astype(BF16)
    normed = (state * inverse_rms(state) * gain_ref[...]).astype(BF16)
    q_ref[...] = dot(normed, w_ref[0]).astype(BF16)
    k_ref[...] = dot(normed, w_ref[1]).astype(BF16)
    v_ref[...] = dot(normed, w_ref[2]).astype(BF16)
    for b in range(2):
        rows = slice(b * BLOCK, (b + 1) * BLOCK)
        for p in range(PAIRS):
            cols = slice(p * 128, (p + 1) * 128)
            scores = compact(dot(k_ref[rows, cols], head_split(q_ref[rows, cols]), NT), 32) * SCALE
            probs = softmax_keys(scores)
            probs_ref[b * PAIRS + p] = probs
            attended = head_join(dot(expand(probs, 32), v_ref[rows, cols], TN))
            attended_ref[rows, cols] = attended.astype(BF16)
    hidden = (state + dot(attended_ref[...], w_ref[3])).astype(BF16)
    hidden = dot(member_major(), hidden).reshape(32, 8, D)
    out_ref[...] = jnp.concatenate([hidden, values[:, 8:]], axis=1).astype(BF16).reshape(8, 4, 16, D)


def window_kernel(
    in_ref, gain_ref, w_ref, out_ref, q_ref, k_ref, v_ref, do_ref, dq_ref, dk_ref, dv_ref
):
    values = in_ref[...].astype(F32)
    hidden = jnp.concatenate([values[:, m, :8].reshape(64, D) for m in range(4)], axis=0)
    dy = jnp.concatenate([values[:, m, 8:].reshape(64, D) for m in range(4)], axis=0)
    inverse = inverse_rms(hidden)
    normed = (hidden * inverse * gain_ref[...]).astype(BF16)
    q_ref[...] = dot(normed, w_ref[0]).astype(BF16)
    k_ref[...] = dot(normed, w_ref[1]).astype(BF16)
    v_ref[...] = dot(normed, w_ref[2]).astype(BF16)
    do_ref[...] = dot(dy.astype(BF16), w_ref[3], NT).astype(BF16)
    for b in range(2):
        rows = slice(b * BLOCK, (b + 1) * BLOCK)
        for p in range(PAIRS):
            cols = slice(p * 128, (p + 1) * 128)
            q_two, do_two = head_split(q_ref[rows, cols]), head_split(do_ref[rows, cols])
            k, v = k_ref[rows, cols], v_ref[rows, cols]
            probs = softmax_keys(compact(dot(k, q_two, NT), 64) * SCALE)
            dq, dk, dv = block_backward(probs, q_two, k, v, do_two, 64)
            dq_ref[rows, cols] = dq.astype(BF16)
            dk_ref[rows, cols] = dk.astype(BF16)
            dv_ref[rows, cols] = dv.astype(BF16)
    upstream = (
        dot(dq_ref[...], w_ref[0], NT) + dot(dk_ref[...], w_ref[1], NT) + dot(dv_ref[...], w_ref[2], NT)
    )
    grad = dy + norm_back(hidden, inverse, gain_ref[...], upstream)
    for m in range(4):
        out_ref[:, m] = grad[m * 64 : (m + 1) * 64].reshape(8, 8, D).astype(BF16)


def member_backward_kernel(
    in_ref, state_ref, q_ref, k_ref, v_ref, probs_ref, gain_ref, w_ref, out_ref, do_ref, dq_ref, dk_ref, dv_ref
):
    values = in_ref[...].astype(F32).reshape(ROWS, D).astype(BF16)
    hidden_grad = dot(cell_major(), values)
    do_ref[...] = dot(hidden_grad.astype(BF16), w_ref[3], NT).astype(BF16)
    for b in range(2):
        rows = slice(b * BLOCK, (b + 1) * BLOCK)
        for p in range(PAIRS):
            cols = slice(p * 128, (p + 1) * 128)
            q_two, do_two = head_split(q_ref[rows, cols]), head_split(do_ref[rows, cols])
            dq, dk, dv = block_backward(
                probs_ref[b * PAIRS + p], q_two, k_ref[rows, cols], v_ref[rows, cols], do_two, 32
            )
            dq_ref[rows, cols] = dq.astype(BF16)
            dk_ref[rows, cols] = dk.astype(BF16)
            dv_ref[rows, cols] = dv.astype(BF16)
    upstream = (
        dot(dq_ref[...], w_ref[0], NT) + dot(dk_ref[...], w_ref[1], NT) + dot(dv_ref[...], w_ref[2], NT)
    )
    state = state_ref[...].astype(F32)
    grad = (hidden_grad + norm_back(state, inverse_rms(state), gain_ref[...], upstream)).astype(BF16)
    out_ref[...] = dot(member_major(), grad).astype(BF16).reshape(32, 8, D)


def call(kernel, outs, scratch=(), flops=0):
    return pl.pallas_call(
        kernel,
        out_shape=outs,
        scratch_shapes=[pltpu.VMEM(s, t) for s, t in scratch],
        compiler_params=pltpu.CompilerParams(vmem_limit_bytes=32 * 1024 * 1024),
    )


def shape(dims, dtype=BF16):
    return jax.ShapeDtypeStruct(dims, dtype)


def member_order():
    def at(y, z):
        return y * 4 + z

    return (
        [at(y, 0) for y in range(8)]
        + [at(y, z) for z in (1, 2) for y in range(4)]
        + [at(y, z) for z in (1, 2) for y in range(4, 8)]
        + [at(y, 3) for y in range(8)]
    )


def groups(patches):
    order = member_order()
    cells = [[m * patches + p for m in order] for p in range(patches)]
    windows = []
    for p in range(patches):
        here, east = cells[p], cells[(p + 1) % patches]
        windows += [here[8:16], here[16:24]]
        windows += [here[24:28] + east[0:4], here[28:32] + east[4:8]]
    return cells, windows


def exchange(array, parties):
    return lax.all_to_all(
        array, ("member", "patch"), 0, 0, axis_index_groups=parties, tiled=True
    )


def body(
    state_field, cotangent, obs_count, member_gain, spatial_gain, member_weights, spatial_weights
):
    cells, windows = groups(lax.axis_size("patch"))
    member_gain, spatial_gain = member_gain.reshape(1, D), spatial_gain.reshape(1, D)
    rows = (ROWS, D)
    sent = call(spread_kernel, shape((32, 16, D)))(
        state_field.reshape(16, 16, D), cotangent.reshape(16, 16, D), obs_count
    )
    at_cells = exchange(sent, cells)
    hidden, state, q, k, v, probs = call(
        member_forward_kernel,
        [shape((8, 4, 16, D))] + [shape(rows)] * 4 + [shape((8, 32, 256), F32)],
        [(rows, BF16)],
    )(at_cells, member_gain, member_weights)
    at_windows = exchange(hidden, windows)
    grads = call(window_kernel, shape((8, 4, 8, D)), [(rows, BF16)] * 7)(
        at_windows, spatial_gain, spatial_weights
    )
    back_at_cells = exchange(grads, windows)
    field = call(member_backward_kernel, shape((32, 8, D)), [(rows, BF16)] * 4)(
        back_at_cells, state, q, k, v, probs, member_gain, member_weights
    )
    returned = exchange(field, cells)
    out = call(gather_kernel, shape((16, 16, D)))(returned)
    return out.reshape(1, 16, 16, D)


def solution(mesh):
    placed = (
        P("member", None, "patch", None),
        P("member", None, "patch", None),
        P(None, "patch"),
        P(),
        P(),
        P(),
        P(),
    )
    return jax.shard_map(
        body,
        mesh=mesh,
        in_specs=placed,
        out_specs=P("member", None, "patch", None),
        check_vma=False,
    )
```

time: 247 us -> 95.2 us (0.39)
  the two profiles are of different devices: /device:TPU:8 before, /device:TPU:7 now
where the time goes in v1:
time: 95.2 us; the launch traced here: 94.6 us
  blocking collectives  82.7 us (87%)
  Pallas kernels  9.13 us (10%)
  local copies, waits for them, and re-layouts  2.76 us (3%)
    all_to_all x4, blocking collectives, exchange(): lax.all_to_all(array, ('member', 'patch'), 0, 0, axis_index_groups=partie...  82.7 us
    pallas_call x1, Pallas kernels, body(): call(window_kernel, shape((8, 4, 8, D)), [(rows, BF16)] * 7)  3.53 us
    pallas_call x1, Pallas kernels, body(): call(member_backward_kernel, shape((32, 8, D)), [(rows, BF16)] * 4)  2.91 us
    unnamed x14, local copies, waits for them, and re-layouts  2.76 us

profile of v1, /device:TPU:7, one launch (start us, length us, event | category | flops | bytes accessed | tf_op | source)
XLA Modules:
  0.0 94.6 jit_solution(16266134316511523476)
XLA Ops:
  0.0 0.0 copy-start
  0.0 0.0 copy-start.2
  0.0 1.1 %copy-done.2 = bf16[1,16,16,512]{3,2,1,0:T(8,128)(2,1)S(1)} copy-done((bf16[1,16,16,512]{3,2,1,0:T(8,128)(2,1)S(1)}, bf16[1,16,16,512]{3,2,1,0:T(8,128)(2,1)}, u32[]{:S(2)}) %copy-start.2) | copy-done | bytes 262168
  1.1 0.0 copy-start.3
  1.1 0.9 %copy-done.3 = bf16[1,16,16,512]{3,2,1,0:T(8,128)(2,1)S(1)} copy-done((bf16[1,16,16,512]{3,2,1,0:T(8,128)(2,1)S(1)}, bf16[1,16,16,512]{3,2,1,0:T(8,128)(2,1)}, u32[]{:S(2)}) %copy-start.3) | copy-done | bytes 262168
  2.1 0.0 copy-start.5
  2.1 0.7 copy-done.5
  2.8 0.0 copy-start.4
  2.8 0.2 shard_map.73
  3.0 29.6 %all_to_all.20.in_ref = bf16[32,16,512]{2,1,0:T(8,128)(2,1)S(1)} all-to-all(bf16[32,16,512]{2,1,0:T(8,128)(2,1)S(1)} %shard_map.73), channel_id=1, replica_groups={{0,64,128,192,256,320,384,448,16,80,144,208,32,96,160,224,272,336,400,4..., dimensions={0} | all-to-all | bytes 1048576 | tf_op jit(solution)/shard_map/all_to_all | solution.py:245
  32.6 0.0 copy-start.1
  32.6 0.0 copy-start.6
  32.6 0.0 copy-done
  32.7 0.0 copy-done.4
  32.7 1.7 %shard_map.74 = (bf16[8,4,16,512]{3,2,1,0:T(8,128)(2,1)S(1)}, bf16[256,512]{1,0:T(8,128)(2,1)S(1)}, bf16[256,512]{1,0:T(8,128)(2,1)S(1)}, bf16[256,512]{1,0:T(8,...) custom-call(bf16[32,16,512]{2,1,0:T(8,128)(2,1)S(1)} %all_to_all.20.in_ref, f32[1,512]{1,0:T(1,128)S(1)} %bitcast.7, ...), custom_call_target="tpu_custom_call" | custom-call | tf_op jit(solution)/shard_map/pallas_call | solution.py:260
  34.4 17.1 %all_to_all.21.in_ref = bf16[8,4,16,512]{3,2,1,0:T(8,128)(2,1)S(1)} all-to-all(bf16[8,4,16,512]{3,2,1,0:T(8,128)(2,1)S(1)} %get-tuple-element.11), channel_id=1, replica_groups={{16,80,144,208,32,96,160,224},{272,336,400,464,288,352,416,480},{48,112..., dimensions={0} | all-to-all | bytes 1048576 | tf_op jit(solution)/shard_map/all_to_all | solution.py:245
  51.5 0.0 copy-done.1
  51.5 0.0 copy-done.6
  51.5 3.5 %shard_map.75 = bf16[8,4,8,512]{3,2,1,0:T(8,128)(2,1)S(1)} custom-call(bf16[8,4,16,512]{3,2,1,0:T(8,128)(2,1)S(1)} %all_to_all.21.in_ref, f32[1,512]{1,0:T(1,128)S(1)} %bitcast.9, bf16[4,512,512]{2,1,0:T(8,128)(2,1)S(1)} %copy-done.1), custom_call_target="tpu_custom_call" | custom-call | tf_op jit(solution)/shard_map/pallas_call | solution.py:266
  55.0 13.7 %all_to_all.22.in_ref = bf16[8,4,8,512]{3,2,1,0:T(8,128)(2,1)S(1)} all-to-all(bf16[8,4,8,512]{3,2,1,0:T(8,128)(2,1)S(1)} %shard_map.75), channel_id=1, replica_groups={{16,80,144,208,32,96,160,224},{272,336,400,464,288,352,416,480},{48,112..., dimensions={0} | all-to-all | bytes 524288 | tf_op jit(solution)/shard_map/all_to_all | solution.py:245
  68.7 2.9 %shard_map.76 = bf16[32,8,512]{2,1,0:T(8,128)(2,1)S(1)} custom-call(bf16[8,4,8,512]{3,2,1,0:T(8,128)(2,1)S(1)} %all_to_all.22.in_ref, bf16[256,512]{1,0:T(8,128)(2,1)S(1)} %get-tuple-element.12.state_ref, bf16[256,512]{1,0:T(8,128)(2,1)S(1)} %get-tuple-element.13.q_ref, bf16[256,512]{1,0:T(8,128)(2,1)S(1)} %get-tuple-element.14.k_ref, ...), custom_call_target="tpu_custom_call" | custom-call | tf_op jit(solution)/shard_map/pallas_call | solution.py:270
  71.6 22.3 %all_to_all.23.in_ref = bf16[32,8,512]{2,1,0:T(8,128)(2,1)S(1)} all-to-all(bf16[32,8,512]{2,1,0:T(8,128)(2,1)S(1)} %shard_map.76), channel_id=1, replica_groups={{0,64,128,192,256,320,384,448,16,80,144,208,32,96,160,224,272,336,400,4..., dimensions={0} | all-to-all | bytes 524288 | tf_op jit(solution)/shard_map/all_to_all | solution.py:245
  93.8 0.8 shard_map.77
Async XLA Ops:
  0.0 32.7 %copy-start = (bf16[4,512,512]{2,1,0:T(8,128)(2,1)S(1)}, bf16[4,512,512]{2,1,0:T(8,128)(2,1)}, u32[]{:S(2)}) copy-start(bf16[4,512,512]{2,1,0:T(8,128)(2,1)} %w_ref.5) | copy-start | bytes 6291460
  0.0 1.1 %copy-start.2 = (bf16[1,16,16,512]{3,2,1,0:T(8,128)(2,1)S(1)}, bf16[1,16,16,512]{3,2,1,0:T(8,128)(2,1)}, u32[]{:S(2)}) copy-start(bf16[1,16,16,512]{3,2,1,0:T(8,128)(2,1)} %param.7) | copy-start | bytes 786436
  1.1 0.9 %copy-start.3 = (bf16[1,16,16,512]{3,2,1,0:T(8,128)(2,1)S(1)}, bf16[1,16,16,512]{3,2,1,0:T(8,128)(2,1)}, u32[]{:S(2)}) copy-start(bf16[1,16,16,512]{3,2,1,0:T(8,128)(2,1)} %param.8) | copy-start | bytes 786436
  2.1 0.7 copy-start.5
  2.8 29.9 %copy-start.4 = (f32[512]{0:T(512)S(1)}, f32[512]{0:T(512)}, u32[]{:S(2)}) copy-start(f32[512]{0:T(512)} %param.10) | copy-start | bytes 6148
  32.6 18.8 %copy-start.1 = (bf16[4,512,512]{2,1,0:T(8,128)(2,1)S(1)}, bf16[4,512,512]{2,1,0:T(8,128)(2,1)}, u32[]{:S(2)}) copy-start(bf16[4,512,512]{2,1,0:T(8,128)(2,1)} %w_ref.4) | copy-start | bytes 6291460
  32.6 18.8 %copy-start.6 = (f32[512]{0:T(512)S(1)}, f32[512]{0:T(512)}, u32[]{:S(2)}) copy-start(f32[512]{0:T(512)} %param.11) | copy-start | bytes 6148

commit v2 on v1

--- a/solution.py
+++ b/solution.py
@@ -81,17 +81,47 @@
     return raised * (1.0 / jnp.sum(raised, axis=0, keepdims=True))
 
 
-def block_backward(probs, q_two, k, v, do_two, size):
-    grad = compact(dot(v, do_two, NT), size)
-    inner = jnp.sum(probs * grad, axis=0, keepdims=True)
-    ds = expand(probs * (grad - inner) * SCALE, size)
-    dv = dot(expand(probs, size), do_two)
-    dk = dot(ds, q_two)
-    dq = head_join(dot(ds, k, TN))
-    return dq, dk, dv
-
-
-def spread_kernel(state_ref, cot_ref, obs_ref, out_ref):
+def blocks():
+    return [
+        (slice(b * BLOCK, (b + 1) * BLOCK), slice(p * 128, (p + 1) * 128))
+        for b in range(ROWS // BLOCK)
+        for p in range(PAIRS)
+    ]
+
+
+def attention_probs(q_split, k_ref, size):
+    scores = [dot(k_ref[at], q, NT) for at, q in zip(blocks(), q_split)]
+    scores = [compact(s, size) * SCALE for s in scores]
+    return [softmax_keys(s) for s in scores]
+
+
+def attention_backward(probs, q_split, k_ref, v_ref, do_split, dq_ref, dk_ref, dv_ref, size):
+    grads = [dot(v_ref[at], do, NT) for at, do in zip(blocks(), do_split)]
+    grads = [compact(g, size) for g in grads]
+    wide = [expand(p, size) for p in probs]
+    ds = [
+        expand(p * (g - jnp.sum(p * g, axis=0, keepdims=True)) * SCALE, size)
+        for p, g in zip(probs, grads)
+    ]
+    for at, p, do in zip(blocks(), wide, do_split):
+        dv_ref[at] = dot(p, do).astype(BF16)
+    for at, d, q in zip(blocks(), ds, q_split):
+        dk_ref[at] = dot(d, q).astype(BF16)
+    for at, d in zip(blocks(), ds):
+        dq_ref[at] = head_join(dot(d, k_ref[at], TN)).astype(BF16)
+
+
+def spread_kernel(state_hbm, cot_hbm, obs_hbm, out_ref, state_ref, cot_ref, obs_ref, sems):
+    copies = [
+        pltpu.make_async_copy(src, dst, sems.at[i])
+        for i, (src, dst) in enumerate(
+            ((obs_hbm, obs_ref), (state_hbm, state_ref), (cot_hbm, cot_ref))
+        )
+    ]
+    for copy in copies:
+        copy.start()
+    for copy in copies:
+        copy.wait()
     obs = obs_ref[...].astype(F32)
     eye = lax.broadcasted_iota(jnp.int32, (16, 16, 16), 1) == lax.broadcasted_iota(
         jnp.int32, (16, 16, 16), 2
@@ -110,12 +140,15 @@
                 jnp.concatenate([east[:, 0], east[:, 1]], axis=1),
             ]
         )
-    for at, size, a, b in zip((0, 8, 24), (8, 16, 8), parts[0], parts[1]):
-        out_ref[at : at + size] = jnp.concatenate([a, b], axis=1).astype(BF16)
+    sent = [jnp.concatenate([a, b], axis=1).astype(BF16) for a, b in zip(parts[0], parts[1])]
+    for k, block in enumerate(block_order()):
+        part, at = (0, block) if block < 8 else (1, block - 8) if block < 24 else (2, block - 24)
+        out_ref[k] = sent[part][at]
 
 
 def gather_kernel(in_ref, out_ref):
-    values = in_ref[...].astype(F32)
+    order = block_order()
+    values = jnp.stack([in_ref[order.index(block)] for block in range(32)]).astype(F32)
     west, east = values[0:8], values[24:32]
     inner = values[8:24].reshape(8, 2, 8, D)
     rows = [
@@ -135,15 +168,11 @@
     q_ref[...] = dot(normed, w_ref[0]).astype(BF16)
     k_ref[...] = dot(normed, w_ref[1]).astype(BF16)
     v_ref[...] = dot(normed, w_ref[2]).astype(BF16)
-    for b in range(2):
-        rows = slice(b * BLOCK, (b + 1) * BLOCK)
-        for p in range(PAIRS):
-            cols = slice(p * 128, (p + 1) * 128)
-            scores = compact(dot(k_ref[rows, cols], head_split(q_ref[rows, cols]), NT), 32) * SCALE
-            probs = softmax_keys(scores)
-            probs_ref[b * PAIRS + p] = probs
-            attended = head_join(dot(expand(probs, 32), v_ref[rows, cols], TN))
-            attended_ref[rows, cols] = attended.astype(BF16)
+    probs = attention_probs([head_split(q_ref[at]) for at in blocks()], k_ref, 32)
+    for i, p in enumerate(probs):
+        probs_ref[i] = p
+    for at, p in zip(blocks(), probs):
+        attended_ref[at] = head_join(dot(expand(p, 32), v_ref[at], TN)).astype(BF16)
     hidden = (state + dot(attended_ref[...], w_ref[3])).astype(BF16)
     hidden = dot(member_major(), hidden).reshape(32, 8, D)
     out_ref[...] = jnp.concatenate([hidden, values[:, 8:]], axis=1).astype(BF16).reshape(8, 4, 16, D)
@@ -161,17 +190,10 @@
     k_ref[...] = dot(normed, w_ref[1]).astype(BF16)
     v_ref[...] = dot(normed, w_ref[2]).astype(BF16)
     do_ref[...] = dot(dy.astype(BF16), w_ref[3], NT).astype(BF16)
-    for b in range(2):
-        rows = slice(b * BLOCK, (b + 1) * BLOCK)
-        for p in range(PAIRS):
-            cols = slice(p * 128, (p + 1) * 128)
-            q_two, do_two = head_split(q_ref[rows, cols]), head_split(do_ref[rows, cols])
-            k, v = k_ref[rows, cols], v_ref[rows, cols]
-            probs = softmax_keys(compact(dot(k, q_two, NT), 64) * SCALE)
-            dq, dk, dv = block_backward(probs, q_two, k, v, do_two, 64)
-            dq_ref[rows, cols] = dq.astype(BF16)
-            dk_ref[rows, cols] = dk.astype(BF16)
-            dv_ref[rows, cols] = dv.astype(BF16)
+    q_split = [head_split(q_ref[at]) for at in blocks()]
+    do_split = [head_split(do_ref[at]) for at in blocks()]
+    probs = attention_probs(q_split, k_ref, 64)
+    attention_backward(probs, q_split, k_ref, v_ref, do_split, dq_ref, dk_ref, dv_ref, 64)
     upstream = (
         dot(dq_ref[...], w_ref[0], NT) + dot(dk_ref[...], w_ref[1], NT) + dot(dv_ref[...], w_ref[2], NT)
     )
@@ -186,17 +208,10 @@
     values = in_ref[...].astype(F32).reshape(ROWS, D).astype(BF16)
     hidden_grad = dot(cell_major(), values)
     do_ref[...] = dot(hidden_grad.astype(BF16), w_ref[3], NT).astype(BF16)
-    for b in range(2):
-        rows = slice(b * BLOCK, (b + 1) * BLOCK)
-        for p in range(PAIRS):
-            cols = slice(p * 128, (p + 1) * 128)
-            q_two, do_two = head_split(q_ref[rows, cols]), head_split(do_ref[rows, cols])
-            dq, dk, dv = block_backward(
-                probs_ref[b * PAIRS + p], q_two, k_ref[rows, cols], v_ref[rows, cols], do_two, 32
-            )
-            dq_ref[rows, cols] = dq.astype(BF16)
-            dk_ref[rows, cols] = dk.astype(BF16)
-            dv_ref[rows, cols] = dv.astype(BF16)
+    q_split = [head_split(q_ref[at]) for at in blocks()]
+    do_split = [head_split(do_ref[at]) for at in blocks()]
+    probs = [probs_ref[i] for i in range(len(q_split))]
+    attention_backward(probs, q_split, k_ref, v_ref, do_split, dq_ref, dk_ref, dv_ref, 32)
     upstream = (
         dot(dq_ref[...], w_ref[0], NT) + dot(dk_ref[...], w_ref[1], NT) + dot(dv_ref[...], w_ref[2], NT)
     )
@@ -205,7 +220,7 @@
     out_ref[...] = dot(member_major(), grad).astype(BF16).reshape(32, 8, D)
 
 
-def call(kernel, outs, scratch=(), flops=0):
+def call(kernel, outs, scratch=()):
     return pl.pallas_call(
         kernel,
         out_shape=outs,
@@ -218,24 +233,38 @@
     return jax.ShapeDtypeStruct(dims, dtype)
 
 
-def member_order():
+def holders():
     def at(y, z):
         return y * 4 + z
 
-    return (
-        [at(y, 0) for y in range(8)]
-        + [at(y, z) for z in (1, 2) for y in range(4)]
-        + [at(y, z) for z in (1, 2) for y in range(4, 8)]
-        + [at(y, 3) for y in range(8)]
-    )
+    west = [at(half + y, z) for half in (0, 4) for y in (0, 1) for z in (0, 1)]
+    within = [at(half + y, z) for half in (0, 4) for y in (2, 3) for z in range(4)]
+    east = [at(half + y, z) for half in (0, 4) for y in (0, 1) for z in (3, 2)]
+    return west + within + east
+
+
+def member_order():
+    order = []
+    for i in range(32):
+        y = (i >> 4 & 1) * 4 + (i >> 3 & 1) * 2 + (i & 1)
+        z = (i >> 1 & 1) * 2 + (i >> 2 & 1)
+        y, z = y ^ (y >> 1), z ^ (z >> 1)
+        order.append(y * 4 + (z + y) % 4)
+    return order
+
+
+def block_order():
+    held = holders()
+    return [held.index(m) for m in member_order()]
 
 
 def groups(patches):
     order = member_order()
     cells = [[m * patches + p for m in order] for p in range(patches)]
+    held = [[m * patches + p for m in holders()] for p in range(patches)]
     windows = []
     for p in range(patches):
-        here, east = cells[p], cells[(p + 1) % patches]
+        here, east = held[p], held[(p + 1) % patches]
         windows += [here[8:16], here[16:24]]
         windows += [here[24:28] + east[0:4], here[28:32] + east[4:8]]
     return cells, windows
@@ -253,9 +282,17 @@
     cells, windows = groups(lax.axis_size("patch"))
     member_gain, spatial_gain = member_gain.reshape(1, D), spatial_gain.reshape(1, D)
     rows = (ROWS, D)
-    sent = call(spread_kernel, shape((32, 16, D)))(
-        state_field.reshape(16, 16, D), cotangent.reshape(16, 16, D), obs_count
-    )
+    sent = pl.pallas_call(
+        spread_kernel,
+        out_shape=shape((32, 16, D)),
+        in_specs=[pl.BlockSpec(memory_space=pltpu.HBM)] * 3,
+        scratch_shapes=[
+            pltpu.VMEM((16, 16, D), BF16),
+            pltpu.VMEM((16, 16, D), BF16),
+            pltpu.VMEM((16, 16), jnp.int32),
+            pltpu.SemaphoreType.DMA((3,)),
+        ],
+    )(state_field.reshape(16, 16, D), cotangent.reshape(16, 16, D), obs_count)
     at_cells = exchange(sent, cells)
     hidden, state, q, k, v, probs = call(
         member_forward_kernel,

time: 95.2 us -> 91.7 us (0.963)
  local copies, waits for them, and re-layouts: 2.76 us -> 0.01 us
    unnamed x14 -> x8, local copies, waits for them, and re-layouts: 2.76 us -> 0.01 us
    pallas_call x1, Pallas kernels: 0.24 us -> 2.24 us  [body(): pl.pallas_call(spread_kernel, out_shape=shape((32, 16, D)), in_specs=[pl....]
    pallas_call x1, Pallas kernels: 3.53 us -> 2.31 us  [body(): call(window_kernel, shape((8, 4, 8, D)), [(rows, BF16)] * 7)]
    pallas_call x1, Pallas kernels: 2.91 us -> 1.94 us  [body(): call(member_backward_kernel, shape((32, 8, D)), [(rows, BF16)] * 4)]
where the time goes in v2:
time: 91.7 us; the launch traced here: 91.4 us
  blocking collectives  82.4 us (90%)
  Pallas kernels  8.89 us (10%)
    all_to_all x4, blocking collectives, exchange(): lax.all_to_all(array, ('member', 'patch'), 0, 0, axis_index_groups=partie...  82.4 us
    pallas_call x1, Pallas kernels, body(): call(window_kernel, shape((8, 4, 8, D)), [(rows, BF16)] * 7)  2.31 us
    pallas_call x1, Pallas kernels, body(): pl.pallas_call(spread_kernel, out_shape=shape((32, 16, D)), in_specs=[pl....  2.24 us
    pallas_call x1, Pallas kernels, body(): call(member_backward_kernel, shape((32, 8, D)), [(rows, BF16)] * 4)  1.94 us

profile of v2, /device:TPU:7, one launch (start us, length us, event | category | flops | bytes accessed | tf_op | source)
XLA Modules:
  0.0 91.4 jit_solution(17842778517712741002)
XLA Ops:
  0.0 0.0 copy-start
  0.0 0.0 copy-start.2
  0.0 2.2 %shard_map.73 = bf16[32,16,512]{2,1,0:T(8,128)(2,1)} custom-call(bf16[16,16,512]{2,1,0:T(8,128)(2,1)} %bitcast.8, bf16[16,16,512]{2,1,0:T(8,128)(2,1)} %bitcast.9, s32[16,16]{1,0:T(8,128)} %obs_hbm.1), custom_call_target="tpu_custom_call" | custom-call | tf_op jit(solution)/shard_map/pallas_call | solution.py:285
  2.3 29.8 %all_to_all.20.in_ref = bf16[32,16,512]{2,1,0:T(8,128)(2,1)S(1)} all-to-all(bf16[32,16,512]{2,1,0:T(8,128)(2,1)} %shard_map.73), channel_id=1, replica_groups={{0,80,48,64,16,96,32,112,240,160,224,144,192,176,208,128,416,496,400,48..., dimensions={0} | all-to-all | bytes 1048576 | tf_op jit(solution)/shard_map/all_to_all | solution.py:274
  32.1 0.0 copy-start.1
  32.1 0.0 copy-start.3
  32.1 0.0 copy-done
  32.1 0.0 copy-done.2
  32.1 1.6 %shard_map.74 = (bf16[8,4,16,512]{3,2,1,0:T(8,128)(2,1)S(1)}, bf16[256,512]{1,0:T(8,128)(2,1)S(1)}, bf16[256,512]{1,0:T(8,128)(2,1)S(1)}, bf16[256,512]{1,0:T(8,...) custom-call(bf16[32,16,512]{2,1,0:T(8,128)(2,1)S(1)} %all_to_all.20.in_ref, f32[1,512]{1,0:T(1,128)S(1)} %bitcast.5, ...), custom_call_target="tpu_custom_call" | custom-call | tf_op jit(solution)/shard_map/pallas_call | solution.py:297
  33.7 16.9 %all_to_all.21.in_ref = bf16[8,4,16,512]{3,2,1,0:T(8,128)(2,1)S(1)} all-to-all(bf16[8,4,16,512]{3,2,1,0:T(8,128)(2,1)S(1)} %get-tuple-element.11), channel_id=1, replica_groups={{128,144,160,176,192,208,224,240},{384,400,416,432,448,464,480,496},{48..., dimensions={0} | all-to-all | bytes 1048576 | tf_op jit(solution)/shard_map/all_to_all | solution.py:274
  50.6 0.0 copy-done.1
  50.6 0.0 copy-done.3
  50.7 2.3 %shard_map.75 = bf16[8,4,8,512]{3,2,1,0:T(8,128)(2,1)S(1)} custom-call(bf16[8,4,16,512]{3,2,1,0:T(8,128)(2,1)S(1)} %all_to_all.21.in_ref, f32[1,512]{1,0:T(1,128)S(1)} %bitcast.7, bf16[4,512,512]{2,1,0:T(8,128)(2,1)S(1)} %copy-done.1), custom_call_target="tpu_custom_call" | custom-call | tf_op jit(solution)/shard_map/pallas_call | solution.py:303
  53.0 12.7 %all_to_all.22.in_ref = bf16[8,4,8,512]{3,2,1,0:T(8,128)(2,1)S(1)} all-to-all(bf16[8,4,8,512]{3,2,1,0:T(8,128)(2,1)S(1)} %shard_map.75), channel_id=1, replica_groups={{128,144,160,176,192,208,224,240},{384,400,416,432,448,464,480,496},{48..., dimensions={0} | all-to-all | bytes 524288 | tf_op jit(solution)/shard_map/all_to_all | solution.py:274
  65.7 1.9 %shard_map.76 = bf16[32,8,512]{2,1,0:T(8,128)(2,1)S(1)} custom-call(bf16[8,4,8,512]{3,2,1,0:T(8,128)(2,1)S(1)} %all_to_all.22.in_ref, bf16[256,512]{1,0:T(8,128)(2,1)S(1)} %get-tuple-element.12.state_ref, bf16[256,512]{1,0:T(8,128)(2,1)S(1)} %get-tuple-element.13.q_ref, bf16[256,512]{1,0:T(8,128)(2,1)S(1)} %get-tuple-element.14.k_ref, ...), custom_call_target="tpu_custom_call" | custom-call | tf_op jit(solution)/shard_map/pallas_call | solution.py:307
  67.7 22.9 %all_to_all.23.in_ref = bf16[32,8,512]{2,1,0:T(8,128)(2,1)S(1)} all-to-all(bf16[32,8,512]{2,1,0:T(8,128)(2,1)S(1)} %shard_map.76), channel_id=1, replica_groups={{0,80,48,64,16,96,32,112,240,160,224,144,192,176,208,128,416,496,400,48..., dimensions={0} | all-to-all | bytes 524288 | tf_op jit(solution)/shard_map/all_to_all | solution.py:274
  90.6 0.8 shard_map.77
Async XLA Ops:
  0.0 32.1 %copy-start = (bf16[4,512,512]{2,1,0:T(8,128)(2,1)S(1)}, bf16[4,512,512]{2,1,0:T(8,128)(2,1)}, u32[]{:S(2)}) copy-start(bf16[4,512,512]{2,1,0:T(8,128)(2,1)} %w_ref.5) | copy-start | bytes 6291460
  0.0 32.1 %copy-start.2 = (f32[512]{0:T(512)S(1)}, f32[512]{0:T(512)}, u32[]{:S(2)}) copy-start(f32[512]{0:T(512)} %param.10) | copy-start | bytes 6148
  32.1 18.6 %copy-start.1 = (bf16[4,512,512]{2,1,0:T(8,128)(2,1)S(1)}, bf16[4,512,512]{2,1,0:T(8,128)(2,1)}, u32[]{:S(2)}) copy-start(bf16[4,512,512]{2,1,0:T(8,128)(2,1)} %w_ref.4) | copy-start | bytes 6291460
  32.1 18.6 %copy-start.3 = (f32[512]{0:T(512)S(1)}, f32[512]{0:T(512)}, u32[]{:S(2)}) copy-start(f32[512]{0:T(512)} %param.11) | copy-start | bytes 6148

commit v3 on v2

--- a/solution.py
+++ b/solution.py
@@ -141,14 +141,13 @@
             ]
         )
     sent = [jnp.concatenate([a, b], axis=1).astype(BF16) for a, b in zip(parts[0], parts[1])]
-    for k, block in enumerate(block_order()):
-        part, at = (0, block) if block < 8 else (1, block - 8) if block < 24 else (2, block - 24)
-        out_ref[k] = sent[part][at]
+    sent = jnp.concatenate(sent, axis=0)
+    for block, at in enumerate(places()):
+        out_ref[at] = sent[block]
 
 
 def gather_kernel(in_ref, out_ref):
-    order = block_order()
-    values = jnp.stack([in_ref[order.index(block)] for block in range(32)]).astype(F32)
+    values = jnp.stack([in_ref[at] for at in places()]).astype(F32)
     west, east = values[0:8], values[24:32]
     inner = values[8:24].reshape(8, 2, 8, D)
     rows = [
@@ -233,35 +232,44 @@
     return jax.ShapeDtypeStruct(dims, dtype)
 
 
-def holders():
+def holders(turned):
     def at(y, z):
         return y * 4 + z
 
-    west = [at(half + y, z) for half in (0, 4) for y in (0, 1) for z in (0, 1)]
-    within = [at(half + y, z) for half in (0, 4) for y in (2, 3) for z in range(4)]
-    east = [at(half + y, z) for half in (0, 4) for y in (0, 1) for z in (3, 2)]
-    return west + within + east
+    inner, outer = ((0, 1), (2, 3)) if turned else ((2, 3), (0, 1))
+    low = [at(half + y, z) for half in (0, 4) for y in outer for z in (0, 1)]
+    high = [at(half + y, z) for half in (0, 4) for y in outer for z in (3, 2)]
+    within = [at(half + y, z) for half in (0, 4) for y in inner for z in range(4)]
+    return high + within + low if turned else low + within + high
+
+
+def is_turned(patch):
+    return patch % 2 == 1, patch % 8 != 7
 
 
 def member_order():
     order = []
     for i in range(32):
-        y = (i >> 4 & 1) * 4 + (i >> 3 & 1) * 2 + (i & 1)
-        z = (i >> 1 & 1) * 2 + (i >> 2 & 1)
-        y, z = y ^ (y >> 1), z ^ (z >> 1)
+        y = (i >> 1 & 1) * 4 + (i >> 2 & 1) * 2 + (i >> 3 & 1)
+        z = (i & 1) * 2 + (i >> 4 & 1)
         order.append(y * 4 + (z + y) % 4)
     return order
 
 
-def block_order():
-    held = holders()
-    return [held.index(m) for m in member_order()]
+def places():
+    order = member_order()
+    odd, near = is_turned(lax.axis_index("patch"))
+    turned = jnp.logical_and(odd, near)
+    return [
+        jnp.where(turned, order.index(there), order.index(here))
+        for here, there in zip(holders(False), holders(True))
+    ]
 
 
 def groups(patches):
     order = member_order()
     cells = [[m * patches + p for m in order] for p in range(patches)]
-    held = [[m * patches + p for m in holders()] for p in range(patches)]
+    held = [[m * patches + p for m in holders(all(is_turned(p)))] for p in range(patches)]
     windows = []
     for p in range(patches):
         here, east = held[p], held[(p + 1) % patches]

time: 91.7 us -> 89 us (0.971)
  blocking collectives: 82.4 us -> 79.8 us
    all_to_all x4, blocking collectives: 82.4 us -> 79.8 us  [exchange(): lax.all_to_all(array, ('member', 'patch'), 0, 0, axis_index_groups=partie...]
where the time goes in v3:
time: 89 us; the launch traced here: 88.6 us
  blocking collectives  79.8 us (90%)
  Pallas kernels  8.82 us (10%)
    all_to_all x4, blocking collectives, exchange(): lax.all_to_all(array, ('member', 'patch'), 0, 0, axis_index_groups=partie...  79.8 us
    pallas_call x1, Pallas kernels, body(): call(window_kernel, shape((8, 4, 8, D)), [(rows, BF16)] * 7)  2.31 us
    pallas_call x1, Pallas kernels, body(): pl.pallas_call(spread_kernel, out_shape=shape((32, 16, D)), in_specs=[pl....  2.18 us
    pallas_call x1, Pallas kernels, body(): call(member_backward_kernel, shape((32, 8, D)), [(rows, BF16)] * 4)  1.94 us

profile of v3, /device:TPU:7, one launch (start us, length us, event | category | flops | bytes accessed | tf_op | source)
XLA Modules:
  0.0 88.6 jit_solution(6886927037113950783)
XLA Ops:
  0.0 0.0 copy-start
  0.0 0.0 copy-start.2
  0.0 2.2 %shard_map.73 = bf16[32,16,512]{2,1,0:T(8,128)(2,1)} custom-call(bf16[16,16,512]{2,1,0:T(8,128)(2,1)} %bitcast.8, bf16[16,16,512]{2,1,0:T(8,128)(2,1)} %bitcast.9, s32[16,16]{1,0:T(8,128)} %obs_hbm.1), custom_call_target="tpu_custom_call" | custom-call | tf_op jit(solution)/shard_map/pallas_call | solution.py:293
  2.2 30.2 %all_to_all.20.in_ref = bf16[32,16,512]{2,1,0:T(8,128)(2,1)S(1)} all-to-all(bf16[32,16,512]{2,1,0:T(8,128)(2,1)} %shard_map.73), channel_id=1, replica_groups={{0,32,256,288,160,128,416,384,80,112,336,368,240,208,496,464,16,48,272,..., dimensions={0} | all-to-all | bytes 1048576 | tf_op jit(solution)/shard_map/all_to_all | solution.py:282
  32.4 0.0 copy-start.1
  32.4 0.0 copy-start.3
  32.4 0.0 copy-done
  32.4 0.0 copy-done.2
  32.4 1.6 %shard_map.74 = (bf16[8,4,16,512]{3,2,1,0:T(8,128)(2,1)S(1)}, bf16[256,512]{1,0:T(8,128)(2,1)S(1)}, bf16[256,512]{1,0:T(8,128)(2,1)S(1)}, bf16[256,512]{1,0:T(8,...) custom-call(bf16[32,16,512]{2,1,0:T(8,128)(2,1)S(1)} %all_to_all.20.in_ref, f32[1,512]{1,0:T(1,128)S(1)} %bitcast.5, ...), custom_call_target="tpu_custom_call" | custom-call | tf_op jit(solution)/shard_map/pallas_call | solution.py:305
  34.1 14.1 %all_to_all.21.in_ref = bf16[8,4,16,512]{3,2,1,0:T(8,128)(2,1)S(1)} all-to-all(bf16[8,4,16,512]{3,2,1,0:T(8,128)(2,1)S(1)} %get-tuple-element.11), channel_id=1, replica_groups={{128,144,160,176,192,208,224,240},{384,400,416,432,448,464,480,496},{48..., dimensions={0} | all-to-all | bytes 1048576 | tf_op jit(solution)/shard_map/all_to_all | solution.py:282
  48.2 0.0 copy-done.1
  48.2 0.0 copy-done.3
  48.2 2.3 %shard_map.75 = bf16[8,4,8,512]{3,2,1,0:T(8,128)(2,1)S(1)} custom-call(bf16[8,4,16,512]{3,2,1,0:T(8,128)(2,1)S(1)} %all_to_all.21.in_ref, f32[1,512]{1,0:T(1,128)S(1)} %bitcast.7, bf16[4,512,512]{2,1,0:T(8,128)(2,1)S(1)} %copy-done.1), custom_call_target="tpu_custom_call" | custom-call | tf_op jit(solution)/shard_map/pallas_call | solution.py:311
  50.5 11.9 %all_to_all.22.in_ref = bf16[8,4,8,512]{3,2,1,0:T(8,128)(2,1)S(1)} all-to-all(bf16[8,4,8,512]{3,2,1,0:T(8,128)(2,1)S(1)} %shard_map.75), channel_id=1, replica_groups={{128,144,160,176,192,208,224,240},{384,400,416,432,448,464,480,496},{48..., dimensions={0} | all-to-all | bytes 524288 | tf_op jit(solution)/shard_map/all_to_all | solution.py:282
  62.4 1.9 %shard_map.76 = bf16[32,8,512]{2,1,0:T(8,128)(2,1)S(1)} custom-call(bf16[8,4,8,512]{3,2,1,0:T(8,128)(2,1)S(1)} %all_to_all.22.in_ref, bf16[256,512]{1,0:T(8,128)(2,1)S(1)} %get-tuple-element.12.state_ref, bf16[256,512]{1,0:T(8,128)(2,1)S(1)} %get-tuple-element.13.q_ref, bf16[256,512]{1,0:T(8,128)(2,1)S(1)} %get-tuple-element.14.k_ref, ...), custom_call_target="tpu_custom_call" | custom-call | tf_op jit(solution)/shard_map/pallas_call | solution.py:315
  64.3 23.6 %all_to_all.23.in_ref = bf16[32,8,512]{2,1,0:T(8,128)(2,1)S(1)} all-to-all(bf16[32,8,512]{2,1,0:T(8,128)(2,1)S(1)} %shard_map.76), channel_id=1, replica_groups={{0,32,256,288,160,128,416,384,80,112,336,368,240,208,496,464,16,48,272,..., dimensions={0} | all-to-all | bytes 524288 | tf_op jit(solution)/shard_map/all_to_all | solution.py:282
  87.9 0.8 shard_map.77
Async XLA Ops:
  0.0 32.4 %copy-start = (bf16[4,512,512]{2,1,0:T(8,128)(2,1)S(1)}, bf16[4,512,512]{2,1,0:T(8,128)(2,1)}, u32[]{:S(2)}) copy-start(bf16[4,512,512]{2,1,0:T(8,128)(2,1)} %w_ref.5) | copy-start | bytes 6291460
  0.0 32.4 %copy-start.2 = (f32[512]{0:T(512)S(1)}, f32[512]{0:T(512)}, u32[]{:S(2)}) copy-start(f32[512]{0:T(512)} %param.10) | copy-start | bytes 6148
  32.4 15.8 %copy-start.1 = (bf16[4,512,512]{2,1,0:T(8,128)(2,1)S(1)}, bf16[4,512,512]{2,1,0:T(8,128)(2,1)}, u32[]{:S(2)}) copy-start(bf16[4,512,512]{2,1,0:T(8,128)(2,1)} %w_ref.4) | copy-start | bytes 6291460
  32.4 15.8 %copy-start.3 = (f32[512]{0:T(512)S(1)}, f32[512]{0:T(512)}, u32[]{:S(2)}) copy-start(f32[512]{0:T(512)} %param.11) | copy-start | bytes 6148

commit v4 on v3

--- a/solution.py
+++ b/solution.py
@@ -248,12 +248,7 @@
 
 
 def member_order():
-    order = []
-    for i in range(32):
-        y = (i >> 1 & 1) * 4 + (i >> 2 & 1) * 2 + (i >> 3 & 1)
-        z = (i & 1) * 2 + (i >> 4 & 1)
-        order.append(y * 4 + (z + y) % 4)
-    return order
+    return [y * 4 + (z + y) % 4 for z in range(4) for y in range(8)]
 
 
 def places():

time: 89 us -> 87.4 us (0.982)
  blocking collectives: 79.8 us -> 78.1 us
    all_to_all x4, blocking collectives: 79.8 us -> 78.1 us  [exchange(): lax.all_to_all(array, ('member', 'patch'), 0, 0, axis_index_groups=partie...]
where the time goes in v4:
time: 87.4 us; the launch traced here: 87 us
  blocking collectives  78.1 us (89%)
  Pallas kernels  8.82 us (10%)
    all_to_all x4, blocking collectives, exchange(): lax.all_to_all(array, ('member', 'patch'), 0, 0, axis_index_groups=partie...  78.1 us
    pallas_call x1, Pallas kernels, body(): call(window_kernel, shape((8, 4, 8, D)), [(rows, BF16)] * 7)  2.31 us
    pallas_call x1, Pallas kernels, body(): pl.pallas_call(spread_kernel, out_shape=shape((32, 16, D)), in_specs=[pl....  2.18 us
    pallas_call x1, Pallas kernels, body(): call(member_backward_kernel, shape((32, 8, D)), [(rows, BF16)] * 4)  1.94 us

profile of v4, /device:TPU:7, one launch (start us, length us, event | category | flops | bytes accessed | tf_op | source)
XLA Modules:
  0.0 87.0 jit_solution(4203328359241843398)
XLA Ops:
  0.0 0.0 copy-start
  0.0 0.0 copy-start.2
  0.0 2.2 %shard_map.73 = bf16[32,16,512]{2,1,0:T(8,128)(2,1)} custom-call(bf16[16,16,512]{2,1,0:T(8,128)(2,1)} %bitcast.8, bf16[16,16,512]{2,1,0:T(8,128)(2,1)} %bitcast.9, s32[16,16]{1,0:T(8,128)} %obs_hbm.1), custom_call_target="tpu_custom_call" | custom-call | tf_op jit(solution)/shard_map/pallas_call | solution.py:288
  2.2 27.4 %all_to_all.20.in_ref = bf16[32,16,512]{2,1,0:T(8,128)(2,1)S(1)} all-to-all(bf16[32,16,512]{2,1,0:T(8,128)(2,1)} %shard_map.73), channel_id=1, replica_groups={{0,80,160,240,256,336,416,496,16,96,176,192,272,352,432,448,32,112,128,..., dimensions={0} | all-to-all | bytes 1048576 | tf_op jit(solution)/shard_map/all_to_all | solution.py:277
  29.6 0.0 copy-start.1
  29.6 0.0 copy-start.3
  29.6 0.0 copy-done
  29.6 0.0 copy-done.2
  29.6 1.6 %shard_map.74 = (bf16[8,4,16,512]{3,2,1,0:T(8,128)(2,1)S(1)}, bf16[256,512]{1,0:T(8,128)(2,1)S(1)}, bf16[256,512]{1,0:T(8,128)(2,1)S(1)}, bf16[256,512]{1,0:T(8,...) custom-call(bf16[32,16,512]{2,1,0:T(8,128)(2,1)S(1)} %all_to_all.20.in_ref, f32[1,512]{1,0:T(1,128)S(1)} %bitcast.5, ...), custom_call_target="tpu_custom_call" | custom-call | tf_op jit(solution)/shard_map/pallas_call | solution.py:300
  31.3 17.2 %all_to_all.21.in_ref = bf16[8,4,16,512]{3,2,1,0:T(8,128)(2,1)S(1)} all-to-all(bf16[8,4,16,512]{3,2,1,0:T(8,128)(2,1)S(1)} %get-tuple-element.11), channel_id=1, replica_groups={{128,144,160,176,192,208,224,240},{384,400,416,432,448,464,480,496},{48..., dimensions={0} | all-to-all | bytes 1048576 | tf_op jit(solution)/shard_map/all_to_all | solution.py:277
  48.5 0.0 copy-done.1
  48.5 0.0 copy-done.3
  48.5 2.3 %shard_map.75 = bf16[8,4,8,512]{3,2,1,0:T(8,128)(2,1)S(1)} custom-call(bf16[8,4,16,512]{3,2,1,0:T(8,128)(2,1)S(1)} %all_to_all.21.in_ref, f32[1,512]{1,0:T(1,128)S(1)} %bitcast.7, bf16[4,512,512]{2,1,0:T(8,128)(2,1)S(1)} %copy-done.1), custom_call_target="tpu_custom_call" | custom-call | tf_op jit(solution)/shard_map/pallas_call | solution.py:306
  50.8 11.3 %all_to_all.22.in_ref = bf16[8,4,8,512]{3,2,1,0:T(8,128)(2,1)S(1)} all-to-all(bf16[8,4,8,512]{3,2,1,0:T(8,128)(2,1)S(1)} %shard_map.75), channel_id=1, replica_groups={{128,144,160,176,192,208,224,240},{384,400,416,432,448,464,480,496},{48..., dimensions={0} | all-to-all | bytes 524288 | tf_op jit(solution)/shard_map/all_to_all | solution.py:277
  62.2 1.9 %shard_map.76 = bf16[32,8,512]{2,1,0:T(8,128)(2,1)S(1)} custom-call(bf16[8,4,8,512]{3,2,1,0:T(8,128)(2,1)S(1)} %all_to_all.22.in_ref, bf16[256,512]{1,0:T(8,128)(2,1)S(1)} %get-tuple-element.12.state_ref, bf16[256,512]{1,0:T(8,128)(2,1)S(1)} %get-tuple-element.13.q_ref, bf16[256,512]{1,0:T(8,128)(2,1)S(1)} %get-tuple-element.14.k_ref, ...), custom_call_target="tpu_custom_call" | custom-call | tf_op jit(solution)/shard_map/pallas_call | solution.py:310
  64.1 22.1 %all_to_all.23.in_ref = bf16[32,8,512]{2,1,0:T(8,128)(2,1)S(1)} all-to-all(bf16[32,8,512]{2,1,0:T(8,128)(2,1)S(1)} %shard_map.76), channel_id=1, replica_groups={{0,80,160,240,256,336,416,496,16,96,176,192,272,352,432,448,32,112,128,..., dimensions={0} | all-to-all | bytes 524288 | tf_op jit(solution)/shard_map/all_to_all | solution.py:277
  86.2 0.8 shard_map.77
Async XLA Ops:
  0.0 29.6 %copy-start = (bf16[4,512,512]{2,1,0:T(8,128)(2,1)S(1)}, bf16[4,512,512]{2,1,0:T(8,128)(2,1)}, u32[]{:S(2)}) copy-start(bf16[4,512,512]{2,1,0:T(8,128)(2,1)} %w_ref.5) | copy-start | bytes 6291460
  0.0 29.6 %copy-start.2 = (f32[512]{0:T(512)S(1)}, f32[512]{0:T(512)}, u32[]{:S(2)}) copy-start(f32[512]{0:T(512)} %param.10) | copy-start | bytes 6148
  29.6 18.9 %copy-start.1 = (bf16[4,512,512]{2,1,0:T(8,128)(2,1)S(1)}, bf16[4,512,512]{2,1,0:T(8,128)(2,1)}, u32[]{:S(2)}) copy-start(bf16[4,512,512]{2,1,0:T(8,128)(2,1)} %w_ref.4) | copy-start | bytes 6291460
  29.6 18.9 %copy-start.3 = (f32[512]{0:T(512)S(1)}, f32[512]{0:T(512)}, u32[]{:S(2)}) copy-start(f32[512]{0:T(512)} %param.11) | copy-start | bytes 6148

commit v5 on v4

--- a/solution.py
+++ b/solution.py
@@ -142,12 +142,12 @@
         )
     sent = [jnp.concatenate([a, b], axis=1).astype(BF16) for a, b in zip(parts[0], parts[1])]
     sent = jnp.concatenate(sent, axis=0)
-    for block, at in enumerate(places()):
+    for block, at in enumerate(places(member_order())):
         out_ref[at] = sent[block]
 
 
 def gather_kernel(in_ref, out_ref):
-    values = jnp.stack([in_ref[at] for at in places()]).astype(F32)
+    values = jnp.stack([in_ref[at] for at in places(return_order())]).astype(F32)
     west, east = values[0:8], values[24:32]
     inner = values[8:24].reshape(8, 2, 8, D)
     rows = [
@@ -216,7 +216,10 @@
     )
     state = state_ref[...].astype(F32)
     grad = (hidden_grad + norm_back(state, inverse_rms(state), gain_ref[...], upstream)).astype(BF16)
-    out_ref[...] = dot(member_major(), grad).astype(BF16).reshape(32, 8, D)
+    grad = dot(member_major(), grad).reshape(32, 8, D).astype(BF16)
+    order = member_order()
+    for k, m in enumerate(return_order()):
+        out_ref[k] = grad[order.index(m)]
 
 
 def call(kernel, outs, scratch=()):
@@ -248,11 +251,14 @@
 
 
 def member_order():
-    return [y * 4 + (z + y) % 4 for z in range(4) for y in range(8)]
-
-
-def places():
-    order = member_order()
+    return [15, 14, 27, 26, 11, 10, 31, 30, 19, 23, 18, 22, 0, 1, 4, 5, 16, 17, 20, 21, 3, 2, 7, 6, 8, 9, 12, 13, 24, 25, 28, 29]
+
+
+def return_order():
+    return [18, 19, 22, 23, 2, 3, 6, 7, 0, 4, 28, 1, 5, 29, 8, 24, 9, 25, 10, 11, 12, 13, 14, 15, 16, 17, 20, 21, 26, 27, 30, 31]
+
+
+def places(order):
     odd, near = is_turned(lax.axis_index("patch"))
     turned = jnp.logical_and(odd, near)
     return [
@@ -262,15 +268,17 @@
 
 
 def groups(patches):
-    order = member_order()
-    cells = [[m * patches + p for m in order] for p in range(patches)]
+    cells, returns = (
+        [[m * patches + p for m in order] for p in range(patches)]
+        for order in (member_order(), return_order())
+    )
     held = [[m * patches + p for m in holders(all(is_turned(p)))] for p in range(patches)]
     windows = []
     for p in range(patches):
         here, east = held[p], held[(p + 1) % patches]
         windows += [here[8:16], here[16:24]]
         windows += [here[24:28] + east[0:4], here[28:32] + east[4:8]]
-    return cells, windows
+    return cells, windows, returns
 
 
 def exchange(array, parties):
@@ -282,7 +290,7 @@
 def body(
     state_field, cotangent, obs_count, member_gain, spatial_gain, member_weights, spatial_weights
 ):
-    cells, windows = groups(lax.axis_size("patch"))
+    cells, windows, returns = groups(lax.axis_size("patch"))
     member_gain, spatial_gain = member_gain.reshape(1, D), spatial_gain.reshape(1, D)
     rows = (ROWS, D)
     sent = pl.pallas_call(
@@ -310,7 +318,7 @@
     field = call(member_backward_kernel, shape((32, 8, D)), [(rows, BF16)] * 4)(
         back_at_cells, state, q, k, v, probs, member_gain, member_weights
     )
-    returned = exchange(field, cells)
+    returned = exchange(field, returns)
     out = call(gather_kernel, shape((16, 16, D)))(returned)
     return out.reshape(1, 16, 16, D)
 

time: 87.4 us -> 84 us (0.961)
  blocking collectives: 78.1 us -> 74.7 us
    all_to_all x4, blocking collectives: 78.1 us -> 74.7 us  [exchange(): lax.all_to_all(array, ('member', 'patch'), 0, 0, axis_index_groups=partie...]
where the time goes in v5:
time: 84 us; the launch traced here: 83.6 us
  blocking collectives  74.7 us (89%)
  Pallas kernels  8.83 us (11%)
    all_to_all x4, blocking collectives, exchange(): lax.all_to_all(array, ('member', 'patch'), 0, 0, axis_index_groups=partie...  74.7 us
    pallas_call x1, Pallas kernels, body(): call(window_kernel, shape((8, 4, 8, D)), [(rows, BF16)] * 7)  2.31 us
    pallas_call x1, Pallas kernels, body(): pl.pallas_call(spread_kernel, out_shape=shape((32, 16, D)), in_specs=[pl....  2.18 us
    pallas_call x1, Pallas kernels, body(): call(member_backward_kernel, shape((32, 8, D)), [(rows, BF16)] * 4)  1.94 us

profile of v5, /device:TPU:7, one launch (start us, length us, event | category | flops | bytes accessed | tf_op | source)
XLA Modules:
  0.0 83.6 jit_solution(2678543267170371291)
XLA Ops:
  0.0 0.0 copy-start
  0.0 0.0 copy-start.2
  0.0 2.2 %shard_map.73 = bf16[32,16,512]{2,1,0:T(8,128)(2,1)} custom-call(bf16[16,16,512]{2,1,0:T(8,128)(2,1)} %bitcast.8, bf16[16,16,512]{2,1,0:T(8,128)(2,1)} %bitcast.9, s32[16,16]{1,0:T(8,128)} %obs_hbm.1), custom_call_target="tpu_custom_call" | custom-call | tf_op jit(solution)/shard_map/pallas_call | solution.py:296
  2.2 26.4 %all_to_all.20.in_ref = bf16[32,16,512]{2,1,0:T(8,128)(2,1)S(1)} all-to-all(bf16[32,16,512]{2,1,0:T(8,128)(2,1)} %shard_map.73), channel_id=1, replica_groups={{240,224,432,416,176,160,496,480,304,368,288,352,0,16,64,80,256,272,320..., dimensions={0} | all-to-all | bytes 1048576 | tf_op jit(solution)/shard_map/all_to_all | solution.py:285
  28.6 0.0 copy-start.1
  28.6 0.0 copy-start.3
  28.6 0.0 copy-done
  28.6 0.0 copy-done.2
  28.6 1.6 %shard_map.74 = (bf16[8,4,16,512]{3,2,1,0:T(8,128)(2,1)S(1)}, bf16[256,512]{1,0:T(8,128)(2,1)S(1)}, bf16[256,512]{1,0:T(8,128)(2,1)S(1)}, bf16[256,512]{1,0:T(8,...) custom-call(bf16[32,16,512]{2,1,0:T(8,128)(2,1)S(1)} %all_to_all.20.in_ref, f32[1,512]{1,0:T(1,128)S(1)} %bitcast.5, ...), custom_call_target="tpu_custom_call" | custom-call | tf_op jit(solution)/shard_map/pallas_call | solution.py:308
  30.2 16.1 %all_to_all.21.in_ref = bf16[8,4,16,512]{3,2,1,0:T(8,128)(2,1)S(1)} all-to-all(bf16[8,4,16,512]{3,2,1,0:T(8,128)(2,1)S(1)} %get-tuple-element.11), channel_id=1, replica_groups={{128,144,160,176,192,208,224,240},{384,400,416,432,448,464,480,496},{48..., dimensions={0} | all-to-all | bytes 1048576 | tf_op jit(solution)/shard_map/all_to_all | solution.py:285
  46.3 0.0 copy-done.1
  46.3 0.0 copy-done.3
  46.3 2.3 %shard_map.75 = bf16[8,4,8,512]{3,2,1,0:T(8,128)(2,1)S(1)} custom-call(bf16[8,4,16,512]{3,2,1,0:T(8,128)(2,1)S(1)} %all_to_all.21.in_ref, f32[1,512]{1,0:T(1,128)S(1)} %bitcast.7, bf16[4,512,512]{2,1,0:T(8,128)(2,1)S(1)} %copy-done.1), custom_call_target="tpu_custom_call" | custom-call | tf_op jit(solution)/shard_map/pallas_call | solution.py:314
  48.6 11.3 %all_to_all.22.in_ref = bf16[8,4,8,512]{3,2,1,0:T(8,128)(2,1)S(1)} all-to-all(bf16[8,4,8,512]{3,2,1,0:T(8,128)(2,1)S(1)} %shard_map.75), channel_id=1, replica_groups={{128,144,160,176,192,208,224,240},{384,400,416,432,448,464,480,496},{48..., dimensions={0} | all-to-all | bytes 524288 | tf_op jit(solution)/shard_map/all_to_all | solution.py:285
  59.9 1.9 %shard_map.76 = bf16[32,8,512]{2,1,0:T(8,128)(2,1)S(1)} custom-call(bf16[8,4,8,512]{3,2,1,0:T(8,128)(2,1)S(1)} %all_to_all.22.in_ref, bf16[256,512]{1,0:T(8,128)(2,1)S(1)} %get-tuple-element.12.state_ref, bf16[256,512]{1,0:T(8,128)(2,1)S(1)} %get-tuple-element.13.q_ref, bf16[256,512]{1,0:T(8,128)(2,1)S(1)} %get-tuple-element.14.k_ref, ...), custom_call_target="tpu_custom_call" | custom-call | tf_op jit(solution)/shard_map/pallas_call | solution.py:318
  61.9 21.0 %all_to_all.23.in_ref = bf16[32,8,512]{2,1,0:T(8,128)(2,1)S(1)} all-to-all(bf16[32,8,512]{2,1,0:T(8,128)(2,1)S(1)} %shard_map.76), channel_id=1, replica_groups={{288,304,352,368,32,48,96,112,0,64,448,16,80,464,128,384,144,400,160,17..., dimensions={0} | all-to-all | bytes 524288 | tf_op jit(solution)/shard_map/all_to_all | solution.py:285
  82.9 0.8 shard_map.77
Async XLA Ops:
  0.0 28.6 %copy-start = (bf16[4,512,512]{2,1,0:T(8,128)(2,1)S(1)}, bf16[4,512,512]{2,1,0:T(8,128)(2,1)}, u32[]{:S(2)}) copy-start(bf16[4,512,512]{2,1,0:T(8,128)(2,1)} %w_ref.5) | copy-start | bytes 6291460
  0.0 28.6 %copy-start.2 = (f32[512]{0:T(512)S(1)}, f32[512]{0:T(512)}, u32[]{:S(2)}) copy-start(f32[512]{0:T(512)} %param.10) | copy-start | bytes 6148
  28.6 17.7 %copy-start.1 = (bf16[4,512,512]{2,1,0:T(8,128)(2,1)S(1)}, bf16[4,512,512]{2,1,0:T(8,128)(2,1)}, u32[]{:S(2)}) copy-start(bf16[4,512,512]{2,1,0:T(8,128)(2,1)} %w_ref.4) | copy-start | bytes 6291460
  28.6 17.7 %copy-start.3 = (f32[512]{0:T(512)S(1)}, f32[512]{0:T(512)}, u32[]{:S(2)}) copy-start(f32[512]{0:T(512)} %param.11) | copy-start | bytes 6148

commit v6 on v5

--- a/solution.py
+++ b/solution.py
@@ -303,7 +303,13 @@
             pltpu.VMEM((16, 16), jnp.int32),
             pltpu.SemaphoreType.DMA((3,)),
         ],
-    )(state_field.reshape(16, 16, D), cotangent.reshape(16, 16, D), obs_count)
+        compiler_params=pltpu.CompilerParams(vmem_limit_bytes=32 * 1024 * 1024),
+    )(
+        *(
+            pltpu.with_memory_space_constraint(array, pltpu.HBM)
+            for array in (state_field.reshape(16, 16, D), cotangent.reshape(16, 16, D), obs_count)
+        )
+    )
     at_cells = exchange(sent, cells)
     hidden, state, q, k, v, probs = call(
         member_forward_kernel,

time: 84 us -> 83 us (0.988)
  no operation moved by 1% of the time
where the time goes in v6:
time: 83 us; the launch traced here: 82.6 us
  blocking collectives  74.5 us (90%)
  Pallas kernels  8.08 us (10%)
    all_to_all x4, blocking collectives, exchange(): lax.all_to_all(array, ('member', 'patch'), 0, 0, axis_index_groups=partie...  74.5 us
    pallas_call x1, Pallas kernels, body(): call(window_kernel, shape((8, 4, 8, D)), [(rows, BF16)] * 7)  2.31 us
    pallas_call x1, Pallas kernels, body(): call(member_backward_kernel, shape((32, 8, D)), [(rows, BF16)] * 4)  1.96 us

profile of v6, /device:TPU:7, one launch (start us, length us, event | category | flops | bytes accessed | tf_op | source)
XLA Modules:
  0.0 82.6 jit_solution(12031825187082994093)
XLA Ops:
  0.0 0.0 copy-start
  0.0 0.0 copy-start.2
  0.0 1.4 %shard_map.73 = bf16[32,16,512]{2,1,0:T(8,128)(2,1)S(1)} custom-call(bf16[16,16,512]{2,1,0:T(8,128)(2,1)} %bitcast.8, bf16[16,16,512]{2,1,0:T(8,128)(2,1)} %bitcast.9, s32[16,16]{1,0:T(8,128)} %obs_hbm.1), custom_call_target="tpu_custom_call" | custom-call | tf_op jit(solution)/shard_map/pallas_call | solution.py:296
  1.4 26.2 %all_to_all.20.in_ref = bf16[32,16,512]{2,1,0:T(8,128)(2,1)S(1)} all-to-all(bf16[32,16,512]{2,1,0:T(8,128)(2,1)S(1)} %shard_map.73), channel_id=1, replica_groups={{240,224,432,416,176,160,496,480,304,368,288,352,0,16,64,80,256,272,320..., dimensions={0} | all-to-all | bytes 1048576 | tf_op jit(solution)/shard_map/all_to_all | solution.py:285
  27.6 0.0 copy-start.1
  27.6 0.0 copy-start.3
  27.6 0.0 copy-done
  27.6 0.0 copy-done.2
  27.6 1.7 %shard_map.74 = (bf16[8,4,16,512]{3,2,1,0:T(8,128)(2,1)S(1)}, bf16[256,512]{1,0:T(8,128)(2,1)S(1)}, bf16[256,512]{1,0:T(8,128)(2,1)S(1)}, bf16[256,512]{1,0:T(8,...) custom-call(bf16[32,16,512]{2,1,0:T(8,128)(2,1)S(1)} %all_to_all.20.in_ref, f32[1,512]{1,0:T(1,128)S(1)} %bitcast.5, ...), custom_call_target="tpu_custom_call" | custom-call | tf_op jit(solution)/shard_map/pallas_call | solution.py:314
  29.2 16.0 %all_to_all.21.in_ref = bf16[8,4,16,512]{3,2,1,0:T(8,128)(2,1)S(1)} all-to-all(bf16[8,4,16,512]{3,2,1,0:T(8,128)(2,1)S(1)} %get-tuple-element.11), channel_id=1, replica_groups={{128,144,160,176,192,208,224,240},{384,400,416,432,448,464,480,496},{48..., dimensions={0} | all-to-all | bytes 1048576 | tf_op jit(solution)/shard_map/all_to_all | solution.py:285
  45.3 0.0 copy-done.1
  45.3 0.0 copy-done.3
  45.3 2.3 %shard_map.75 = bf16[8,4,8,512]{3,2,1,0:T(8,128)(2,1)S(1)} custom-call(bf16[8,4,16,512]{3,2,1,0:T(8,128)(2,1)S(1)} %all_to_all.21.in_ref, f32[1,512]{1,0:T(1,128)S(1)} %bitcast.7, bf16[4,512,512]{2,1,0:T(8,128)(2,1)S(1)} %copy-done.1), custom_call_target="tpu_custom_call" | custom-call | tf_op jit(solution)/shard_map/pallas_call | solution.py:320
  47.6 11.3 %all_to_all.22.in_ref = bf16[8,4,8,512]{3,2,1,0:T(8,128)(2,1)S(1)} all-to-all(bf16[8,4,8,512]{3,2,1,0:T(8,128)(2,1)S(1)} %shard_map.75), channel_id=1, replica_groups={{128,144,160,176,192,208,224,240},{384,400,416,432,448,464,480,496},{48..., dimensions={0} | all-to-all | bytes 524288 | tf_op jit(solution)/shard_map/all_to_all | solution.py:285
  58.9 2.0 %shard_map.76 = bf16[32,8,512]{2,1,0:T(8,128)(2,1)S(1)} custom-call(bf16[8,4,8,512]{3,2,1,0:T(8,128)(2,1)S(1)} %all_to_all.22.in_ref, bf16[256,512]{1,0:T(8,128)(2,1)S(1)} %get-tuple-element.12.state_ref, bf16[256,512]{1,0:T(8,128)(2,1)S(1)} %get-tuple-element.13.q_ref, bf16[256,512]{1,0:T(8,128)(2,1)S(1)} %get-tuple-element.14.k_ref, ...), custom_call_target="tpu_custom_call" | custom-call | tf_op jit(solution)/shard_map/pallas_call | solution.py:324
  60.9 21.0 %all_to_all.23.in_ref = bf16[32,8,512]{2,1,0:T(8,128)(2,1)S(1)} all-to-all(bf16[32,8,512]{2,1,0:T(8,128)(2,1)S(1)} %shard_map.76), channel_id=1, replica_groups={{288,304,352,368,32,48,96,112,0,64,448,16,80,464,128,384,144,400,160,17..., dimensions={0} | all-to-all | bytes 524288 | tf_op jit(solution)/shard_map/all_to_all | solution.py:285
  81.9 0.8 shard_map.77
Async XLA Ops:
  0.0 27.6 %copy-start = (bf16[4,512,512]{2,1,0:T(8,128)(2,1)S(1)}, bf16[4,512,512]{2,1,0:T(8,128)(2,1)}, u32[]{:S(2)}) copy-start(bf16[4,512,512]{2,1,0:T(8,128)(2,1)} %w_ref.5) | copy-start | bytes 6291460
  0.0 27.6 %copy-start.2 = (f32[512]{0:T(512)S(1)}, f32[512]{0:T(512)}, u32[]{:S(2)}) copy-start(f32[512]{0:T(512)} %param.10) | copy-start | bytes 6148
  27.6 17.7 %copy-start.1 = (bf16[4,512,512]{2,1,0:T(8,128)(2,1)S(1)}, bf16[4,512,512]{2,1,0:T(8,128)(2,1)}, u32[]{:S(2)}) copy-start(bf16[4,512,512]{2,1,0:T(8,128)(2,1)} %w_ref.4) | copy-start | bytes 6291460
  27.6 17.7 %copy-start.3 = (f32[512]{0:T(512)S(1)}, f32[512]{0:T(512)}, u32[]{:S(2)}) copy-start(f32[512]{0:T(512)} %param.11) | copy-start | bytes 6148

commit v7 on v6

--- a/solution.py
+++ b/solution.py
@@ -251,7 +251,7 @@
 
 
 def member_order():
-    return [15, 14, 27, 26, 11, 10, 31, 30, 19, 23, 18, 22, 0, 1, 4, 5, 16, 17, 20, 21, 3, 2, 7, 6, 8, 9, 12, 13, 24, 25, 28, 29]
+    return [15, 27, 11, 31, 14, 26, 10, 30, 19, 23, 18, 22, 4, 0, 5, 1, 20, 16, 21, 17, 7, 3, 6, 2, 8, 9, 12, 13, 24, 25, 28, 29]
 
 
 def return_order():

time: 83 us -> 83 us (level)
  no operation moved by 1% of the time
where the time goes in v7:
time: 83 us; the launch traced here: 82.7 us
  blocking collectives  74.6 us (90%)
  Pallas kernels  8.06 us (10%)
    all_to_all x4, blocking collectives, exchange(): lax.all_to_all(array, ('member', 'patch'), 0, 0, axis_index_groups=partie...  74.6 us
    pallas_call x1, Pallas kernels, body(): call(window_kernel, shape((8, 4, 8, D)), [(rows, BF16)] * 7)  2.31 us
    pallas_call x1, Pallas kernels, body(): call(member_backward_kernel, shape((32, 8, D)), [(rows, BF16)] * 4)  1.96 us

profile of v7, /device:TPU:7, one launch (start us, length us, event | category | flops | bytes accessed | tf_op | source)
XLA Modules:
  0.0 82.7 jit_solution(8963835384782416708)
XLA Ops:
  0.0 0.0 copy-start
  0.0 0.0 copy-start.2
  0.0 1.4 %shard_map.73 = bf16[32,16,512]{2,1,0:T(8,128)(2,1)S(1)} custom-call(bf16[16,16,512]{2,1,0:T(8,128)(2,1)} %bitcast.8, bf16[16,16,512]{2,1,0:T(8,128)(2,1)} %bitcast.9, s32[16,16]{1,0:T(8,128)} %obs_hbm.1), custom_call_target="tpu_custom_call" | custom-call | tf_op jit(solution)/shard_map/pallas_call | solution.py:296
  1.4 26.9 %all_to_all.20.in_ref = bf16[32,16,512]{2,1,0:T(8,128)(2,1)S(1)} all-to-all(bf16[32,16,512]{2,1,0:T(8,128)(2,1)S(1)} %shard_map.73), channel_id=1, replica_groups={{240,432,176,496,224,416,160,480,304,368,288,352,64,0,80,16,320,256,336..., dimensions={0} | all-to-all | bytes 1048576 | tf_op jit(solution)/shard_map/all_to_all | solution.py:285
  28.3 0.0 copy-start.1
  28.3 0.0 copy-start.3
  28.3 0.0 copy-done
  28.3 0.0 copy-done.2
  28.3 1.6 %shard_map.74 = (bf16[8,4,16,512]{3,2,1,0:T(8,128)(2,1)S(1)}, bf16[256,512]{1,0:T(8,128)(2,1)S(1)}, bf16[256,512]{1,0:T(8,128)(2,1)S(1)}, bf16[256,512]{1,0:T(8,...) custom-call(bf16[32,16,512]{2,1,0:T(8,128)(2,1)S(1)} %all_to_all.20.in_ref, f32[1,512]{1,0:T(1,128)S(1)} %bitcast.5, ...), custom_call_target="tpu_custom_call" | custom-call | tf_op jit(solution)/shard_map/pallas_call | solution.py:314
  29.9 15.5 %all_to_all.21.in_ref = bf16[8,4,16,512]{3,2,1,0:T(8,128)(2,1)S(1)} all-to-all(bf16[8,4,16,512]{3,2,1,0:T(8,128)(2,1)S(1)} %get-tuple-element.11), channel_id=1, replica_groups={{128,144,160,176,192,208,224,240},{384,400,416,432,448,464,480,496},{48..., dimensions={0} | all-to-all | bytes 1048576 | tf_op jit(solution)/shard_map/all_to_all | solution.py:285
  45.5 0.0 copy-done.1
  45.5 0.0 copy-done.3
  45.5 2.3 %shard_map.75 = bf16[8,4,8,512]{3,2,1,0:T(8,128)(2,1)S(1)} custom-call(bf16[8,4,16,512]{3,2,1,0:T(8,128)(2,1)S(1)} %all_to_all.21.in_ref, f32[1,512]{1,0:T(1,128)S(1)} %bitcast.7, bf16[4,512,512]{2,1,0:T(8,128)(2,1)S(1)} %copy-done.1), custom_call_target="tpu_custom_call" | custom-call | tf_op jit(solution)/shard_map/pallas_call | solution.py:320
  47.8 11.3 %all_to_all.22.in_ref = bf16[8,4,8,512]{3,2,1,0:T(8,128)(2,1)S(1)} all-to-all(bf16[8,4,8,512]{3,2,1,0:T(8,128)(2,1)S(1)} %shard_map.75), channel_id=1, replica_groups={{128,144,160,176,192,208,224,240},{384,400,416,432,448,464,480,496},{48..., dimensions={0} | all-to-all | bytes 524288 | tf_op jit(solution)/shard_map/all_to_all | solution.py:285
  59.1 2.0 %shard_map.76 = bf16[32,8,512]{2,1,0:T(8,128)(2,1)S(1)} custom-call(bf16[8,4,8,512]{3,2,1,0:T(8,128)(2,1)S(1)} %all_to_all.22.in_ref, bf16[256,512]{1,0:T(8,128)(2,1)S(1)} %get-tuple-element.12.state_ref, bf16[256,512]{1,0:T(8,128)(2,1)S(1)} %get-tuple-element.13.q_ref, bf16[256,512]{1,0:T(8,128)(2,1)S(1)} %get-tuple-element.14.k_ref, ...), custom_call_target="tpu_custom_call" | custom-call | tf_op jit(solution)/shard_map/pallas_call | solution.py:324
  61.1 20.8 %all_to_all.23.in_ref = bf16[32,8,512]{2,1,0:T(8,128)(2,1)S(1)} all-to-all(bf16[32,8,512]{2,1,0:T(8,128)(2,1)S(1)} %shard_map.76), channel_id=1, replica_groups={{288,304,352,368,32,48,96,112,0,64,448,16,80,464,128,384,144,400,160,17..., dimensions={0} | all-to-all | bytes 524288 | tf_op jit(solution)/shard_map/all_to_all | solution.py:285
  81.9 0.8 shard_map.77
Async XLA Ops:
  0.0 28.3 %copy-start = (bf16[4,512,512]{2,1,0:T(8,128)(2,1)S(1)}, bf16[4,512,512]{2,1,0:T(8,128)(2,1)}, u32[]{:S(2)}) copy-start(bf16[4,512,512]{2,1,0:T(8,128)(2,1)} %w_ref.5) | copy-start | bytes 6291460
  0.0 28.3 %copy-start.2 = (f32[512]{0:T(512)S(1)}, f32[512]{0:T(512)}, u32[]{:S(2)}) copy-start(f32[512]{0:T(512)} %param.10) | copy-start | bytes 6148
  28.3 17.2 %copy-start.1 = (bf16[4,512,512]{2,1,0:T(8,128)(2,1)S(1)}, bf16[4,512,512]{2,1,0:T(8,128)(2,1)}, u32[]{:S(2)}) copy-start(bf16[4,512,512]{2,1,0:T(8,128)(2,1)} %w_ref.4) | copy-start | bytes 6291460
  28.3 17.2 %copy-start.3 = (f32[512]{0:T(512)S(1)}, f32[512]{0:T(512)}, u32[]{:S(2)}) copy-start(f32[512]{0:T(512)} %param.11) | copy-start | bytes 6148

commit v8 on v7

--- a/solution.py
+++ b/solution.py
@@ -120,16 +120,18 @@
     ]
     for copy in copies:
         copy.start()
-    for copy in copies:
-        copy.wait()
+    copies[0].wait()
     obs = obs_ref[...].astype(F32)
     eye = lax.broadcasted_iota(jnp.int32, (16, 16, 16), 1) == lax.broadcasted_iota(
         jnp.int32, (16, 16, 16), 2
     )
     weight = jnp.sum(jnp.where(eye, obs[:, None, :], 0.0), axis=-1, keepdims=True)
-    dy = cot_ref[...].astype(F32) * weight
     parts = []
-    for values in (state_ref[...].astype(F32), dy):
+    for ref, copy, scale in ((state_ref, copies[1], None), (cot_ref, copies[2], weight)):
+        copy.wait()
+        values = ref[...].astype(F32)
+        if scale is not None:
+            values = values * scale
         inner = values[:, 4:12]
         west = values[:, 0:4].reshape(8, 2, 4, D)
         east = values[:, 12:16].reshape(8, 2, 4, D)
@@ -277,7 +279,9 @@
     for p in range(patches):
         here, east = held[p], held[(p + 1) % patches]
         windows += [here[8:16], here[16:24]]
-        windows += [here[24:28] + east[0:4], here[28:32] + east[4:8]]
+        for half in (0, 4):
+            both = here[24 + half : 28 + half], east[half : half + 4]
+            windows.append([group[i] for group in both for i in (1, 3, 0, 2)])
     return cells, windows, returns
 
 

time: 83 us -> 82.8 us (level)
  no operation moved by 1% of the time
where the time goes in v8:
time: 82.8 us; the launch traced here: 82.5 us
  blocking collectives  74.5 us (90%)
  Pallas kernels  8 us (10%)
    all_to_all x4, blocking collectives, exchange(): lax.all_to_all(array, ('member', 'patch'), 0, 0, axis_index_groups=partie...  74.5 us
    pallas_call x1, Pallas kernels, body(): call(window_kernel, shape((8, 4, 8, D)), [(rows, BF16)] * 7)  2.3 us
    pallas_call x1, Pallas kernels, body(): call(member_backward_kernel, shape((32, 8, D)), [(rows, BF16)] * 4)  1.96 us

profile of v8, /device:TPU:7, one launch (start us, length us, event | category | flops | bytes accessed | tf_op | source)
XLA Modules:
  0.0 82.5 jit_solution(11514182065459067213)
XLA Ops:
  0.0 0.0 copy-start
  0.0 0.0 copy-start.2
  0.0 1.3 %shard_map.73 = bf16[32,16,512]{2,1,0:T(8,128)(2,1)S(1)} custom-call(bf16[16,16,512]{2,1,0:T(8,128)(2,1)} %bitcast.8, bf16[16,16,512]{2,1,0:T(8,128)(2,1)} %bitcast.9, s32[16,16]{1,0:T(8,128)} %obs_hbm.1), custom_call_target="tpu_custom_call" | custom-call | tf_op jit(solution)/shard_map/pallas_call | solution.py:300
  1.4 26.9 %all_to_all.20.in_ref = bf16[32,16,512]{2,1,0:T(8,128)(2,1)S(1)} all-to-all(bf16[32,16,512]{2,1,0:T(8,128)(2,1)S(1)} %shard_map.73), channel_id=1, replica_groups={{240,432,176,496,224,416,160,480,304,368,288,352,64,0,80,16,320,256,336..., dimensions={0} | all-to-all | bytes 1048576 | tf_op jit(solution)/shard_map/all_to_all | solution.py:289
  28.2 0.0 copy-start.1
  28.2 0.0 copy-start.3
  28.2 0.0 copy-done
  28.2 0.0 copy-done.2
  28.3 1.6 %shard_map.74 = (bf16[8,4,16,512]{3,2,1,0:T(8,128)(2,1)S(1)}, bf16[256,512]{1,0:T(8,128)(2,1)S(1)}, bf16[256,512]{1,0:T(8,128)(2,1)S(1)}, bf16[256,512]{1,0:T(8,...) custom-call(bf16[32,16,512]{2,1,0:T(8,128)(2,1)S(1)} %all_to_all.20.in_ref, f32[1,512]{1,0:T(1,128)S(1)} %bitcast.5, ...), custom_call_target="tpu_custom_call" | custom-call | tf_op jit(solution)/shard_map/pallas_call | solution.py:318
  29.9 14.5 %all_to_all.21.in_ref = bf16[8,4,16,512]{3,2,1,0:T(8,128)(2,1)S(1)} all-to-all(bf16[8,4,16,512]{3,2,1,0:T(8,128)(2,1)S(1)} %get-tuple-element.11), channel_id=1, replica_groups={{128,144,160,176,192,208,224,240},{384,400,416,432,448,464,480,496},{32..., dimensions={0} | all-to-all | bytes 1048576 | tf_op jit(solution)/shard_map/all_to_all | solution.py:289
  44.4 0.0 copy-done.1
  44.4 0.0 copy-done.3
  44.4 2.3 %shard_map.75 = bf16[8,4,8,512]{3,2,1,0:T(8,128)(2,1)S(1)} custom-call(bf16[8,4,16,512]{3,2,1,0:T(8,128)(2,1)S(1)} %all_to_all.21.in_ref, f32[1,512]{1,0:T(1,128)S(1)} %bitcast.7, bf16[4,512,512]{2,1,0:T(8,128)(2,1)S(1)} %copy-done.1), custom_call_target="tpu_custom_call" | custom-call | tf_op jit(solution)/shard_map/pallas_call | solution.py:324
  46.7 12.0 %all_to_all.22.in_ref = bf16[8,4,8,512]{3,2,1,0:T(8,128)(2,1)S(1)} all-to-all(bf16[8,4,8,512]{3,2,1,0:T(8,128)(2,1)S(1)} %shard_map.75), channel_id=1, replica_groups={{128,144,160,176,192,208,224,240},{384,400,416,432,448,464,480,496},{32..., dimensions={0} | all-to-all | bytes 524288 | tf_op jit(solution)/shard_map/all_to_all | solution.py:289
  58.6 2.0 %shard_map.76 = bf16[32,8,512]{2,1,0:T(8,128)(2,1)S(1)} custom-call(bf16[8,4,8,512]{3,2,1,0:T(8,128)(2,1)S(1)} %all_to_all.22.in_ref, bf16[256,512]{1,0:T(8,128)(2,1)S(1)} %get-tuple-element.12.state_ref, bf16[256,512]{1,0:T(8,128)(2,1)S(1)} %get-tuple-element.13.q_ref, bf16[256,512]{1,0:T(8,128)(2,1)S(1)} %get-tuple-element.14.k_ref, ...), custom_call_target="tpu_custom_call" | custom-call | tf_op jit(solution)/shard_map/pallas_call | solution.py:328
  60.6 21.2 %all_to_all.23.in_ref = bf16[32,8,512]{2,1,0:T(8,128)(2,1)S(1)} all-to-all(bf16[32,8,512]{2,1,0:T(8,128)(2,1)S(1)} %shard_map.76), channel_id=1, replica_groups={{288,304,352,368,32,48,96,112,0,64,448,16,80,464,128,384,144,400,160,17..., dimensions={0} | all-to-all | bytes 524288 | tf_op jit(solution)/shard_map/all_to_all | solution.py:289
  81.8 0.8 shard_map.77
Async XLA Ops:
  0.0 28.2 %copy-start = (bf16[4,512,512]{2,1,0:T(8,128)(2,1)S(1)}, bf16[4,512,512]{2,1,0:T(8,128)(2,1)}, u32[]{:S(2)}) copy-start(bf16[4,512,512]{2,1,0:T(8,128)(2,1)} %w_ref.5) | copy-start | bytes 6291460
  0.0 28.2 %copy-start.2 = (f32[512]{0:T(512)S(1)}, f32[512]{0:T(512)}, u32[]{:S(2)}) copy-start(f32[512]{0:T(512)} %param.10) | copy-start | bytes 6148
  28.2 16.1 %copy-start.1 = (bf16[4,512,512]{2,1,0:T(8,128)(2,1)S(1)}, bf16[4,512,512]{2,1,0:T(8,128)(2,1)}, u32[]{:S(2)}) copy-start(bf16[4,512,512]{2,1,0:T(8,128)(2,1)} %w_ref.4) | copy-start | bytes 6291460
  28.2 16.1 %copy-start.3 = (f32[512]{0:T(512)S(1)}, f32[512]{0:T(512)}, u32[]{:S(2)}) copy-start(f32[512]{0:T(512)} %param.11) | copy-start | bytes 6148
